TPU v7x, 256 devices: a whole 4x4x8 slice. The times are simulated.
256 devices in a mesh: feat: 128 (over z, y, x), rel: 2 (over core).
Axes of the slice: x: 4, y: 4, z: 8, core: 2. Of those that a mesh axis runs over, the one named last changes fastest.
Arguments:
- features: bfloat16 [768, 16384], P(None, 'feat'), may hold values from -6 to 6
- rel_weight: bfloat16 [4, 768, 768], P('rel'), may hold values from -0.21875 to 0.21875
- self_weight: bfloat16 [768, 768], P('rel'), may hold values from -0.21875 to 0.21875
- block_rows: int32 [4, 64], P('rel'), may hold values from 0 to 127
- block_cols: int32 [4, 64], P('rel'), may hold values from 0 to 127, as said below
- count_tiles: int32 [4, 64, 128, 128], P('rel'), may hold values from 0 to 3
- live_slots: int32 [4], P('rel'), may hold values from 32 to 64, as said below
- degrees: int32 [4, 16384], P('rel', 'feat'), may hold values from 16 to 127
Outputs:
- mixed: bfloat16 [768, 16384], P(None, 'feat')
Inputs may be any that keep to these rules, and one draw needn't show every extreme that they name: Slots at or beyond live_slots[r] are unused; at least 32 slots of each relation are used, one relation uses all 64 and one exactly 32. `block_cols`: over the first 32 slots of all relations together every source block occurs.
All inputs are finite; a program needn't handle non-finite values.
Results may differ from a plain program's by a relative error of at most 0.0034.
Values may be sent and summed in bfloat16 or wider, within the bound.
No kernel may reach another device: no remote copies, remote signals or barrier semaphores. Data moves between devices by JAX's collectives and lax.ppermute only.
A program may use at most 64 MiB of HBM per device.

v0:
```python
import jax
import jax.numpy as jnp
from jax import lax
from jax.sharding import PartitionSpec as P


def relation_blocks(blocked, rows_k, cols_k, tiles_k, count_k):
    block_count = blocked.shape[0]
    col_width = blocked.shape[1]
    block_size = blocked.shape[2]
    slot_count = rows_k.shape[0]
    slot_ids = jnp.arange(slot_count, dtype=jnp.int32)
    active = slot_ids < count_k
    tile_group = jnp.where(active[:, None, None], tiles_k, 0).astype(jnp.bfloat16)
    panels = jnp.take(blocked, cols_k, axis=0)
    contrib = jnp.einsum("sdj,sij->sdi", panels, tile_group, preferred_element_type=jnp.float32)
    block_ids = jnp.arange(block_count, dtype=jnp.int32)
    placing = (block_ids[:, None] == rows_k[None, :]).astype(jnp.float32)
    placed = jnp.dot(
        placing,
        contrib.reshape(slot_count, col_width * block_size),
        precision=lax.Precision.HIGHEST,
        preferred_element_type=jnp.float32,
    )
    return placed.reshape(block_count, col_width, block_size)


def shards(
    features, rel_weight, self_weight, block_rows, block_cols, count_tiles, live_slots, degrees
):
    width_all = features.shape[0]
    node_local = features.shape[1]
    block_size = count_tiles.shape[2]
    local_blocks = node_local // block_size
    grouped = jnp.transpose(features.reshape(width_all, local_blocks, block_size), (1, 0, 2))
    blocked = lax.all_to_all(grouped, "feat", split_axis=1, concat_axis=0, tiled=True)
    stacked = jnp.stack(
        [
            relation_blocks(
                blocked,
                block_rows[relation],
                block_cols[relation],
                count_tiles[relation],
                live_slots[relation],
            )
            for relation in range(block_rows.shape[0])
        ]
    )
    gathered = lax.all_to_all(stacked, "feat", split_axis=1, concat_axis=2, tiled=True)
    scale_local = degrees.astype(jnp.float32).reshape(degrees.shape[0], local_blocks, 1, block_size)
    hidden = (gathered / scale_local).astype(jnp.bfloat16)
    partial_sum = jnp.einsum(
        "kbdi,kde->ebi", hidden, rel_weight, preferred_element_type=jnp.float32
    ).reshape(width_all, node_local)
    half_rows = self_weight.shape[0]
    self_part = lax.dynamic_slice_in_dim(features, lax.axis_index("rel") * half_rows, half_rows, 0)
    partial_sum = partial_sum + lax.dot_general(
        self_weight, self_part, (((0,), (0,)), ((), ())), preferred_element_type=jnp.float32
    )
    total_sum = lax.psum(partial_sum, "rel")
    mixed = jnp.maximum(total_sum, 0.0).astype(jnp.bfloat16)
    return mixed


def solution(mesh):
    placed = (
        P(None, "feat"),
        P("rel", None, None),
        P("rel", None),
        P("rel", None),
        P("rel", None),
        P("rel", None, None, None),
        P("rel"),
        P("rel", "feat"),
    )
    return jax.shard_map(
        shards, mesh=mesh, in_specs=placed, out_specs=P(None, "feat"), check_vma=False
    )
```

profile of v0, /device:TPU:1, one launch (start us, length us, event | category | flops | bytes accessed | tf_op | source)
XLA Modules:
  0.0 84.8 jit_solution(16949558730216719400)
XLA Ops:
  0.0 0.0 copy-start
  0.0 1.4 %copy.56 = bf16[1,768,128]{2,0,1:T(2,128)(2,1)S(1)} copy(bf16[1,768,128]{2,1,0:T(8,128)(2,1)} %bitcast.81) | data formatting | bytes 393216 | tf_op jit(solution)/shard_map/transpose;reshape | solution.py:35
  1.4 0.5 broadcast.95
  1.9 1.8 %reduce.2 = bf16[768,128]{1,0:T(8,128)(2,1)S(1)} reduce(bf16[768,1,128]{2,1,0:T(2,128)(2,1)S(1)} %bitcast.78, bf16[]{:T(256)} %broadcast.95), dimensions={1}, to_apply=%bitcast.77.reduce_sub_computation | reduce | bytes 393218
  3.7 0.8 reshape.184
  4.5 16.3 %all-to-all-start = ((bf16[128,2,384]{2,1,0:T(2,128)(2,1)}), bf16[128,2,384]{2,1,0:T(2,128)(2,1)S(1)}, u32[]{:S(2)}, u32[]{:S(2)}) async-start(bf16[128,2,384]{2,1,0:T(2,128)(2,1)} %reshape.184), calls=%async_computation | async-start | bytes 393216 | tf_op jit(solution)/shard_map/all_to_all | solution.py:36
  20.8 0.8 compare_and_fusion.1
  21.6 1.3 %fusion.35 = (s32[1]{0:T(128)}, s32[1]{0:T(128)}) fusion(s32[2]{0:T(128)} %param.16), kind=kLoop, calls=%fused_computation.56 | loop fusion | bytes 16 | tf_op jit(solution)/shard_map/slice | solution.py:44
  22.9 0.6 iota_compare_fusion.3
  23.5 0.6 iota_compare_fusion.2
  24.2 0.8 slice_bitcast_fusion.1
  25.0 7.8 %all-to-all-done = bf16[128,2,384]{2,1,0:T(2,128)(2,1)S(1)} async-done(((bf16[128,2,384]{2,1,0:T(2,128)(2,1)}), bf16[128,2,384]{2,1,0:T(2,128)(2,1)S(1)}, u32[]{:S(2)}, u32[]{:S(2)}) %all-to-all-start) | async-done | bytes 196640 | tf_op jit(solution)/shard_map/all_to_all | solution.py:36
  32.8 0.1 reshape.185
  32.9 1.1 %bitcast_reduce_fusion = bf16[768,128]{1,0:T(8,128)(2,1)S(1)} fusion(bf16[768,1,128]{2,1,0:T(2,128)(2,1)S(1)} %reshape.185), kind=kLoop, calls=%fused_computation.57 | loop fusion | bytes 393216 | tf_op jit(solution)/shard_map/all_to_all | solution.py:36
  34.0 0.1 all_to_all.9
  34.1 0.6 gather_fusion
  34.7 0.6 gather_fusion.1
  35.4 3.4 %fusion.2 = f32[64,6,128]{2,1,0:T(8,128)S(1)} fusion(s32[2,64,128,128]{3,2,1,0:T(8,128)} %param.15, pred[64]{0:T(512)(128)(4,1)S(1)} %iota_compare_fusion.3, bf16[64,6,128]{2,1,0:T(8,128)(2,1)S(1)} %gather_fusion, pred[64]{0:T(512)(128)(4,1)S(1)} %get-tuple-element.6), kind=kOutput, calls=%fused_computation.6 | convolution fusion | flops 14729216 | bytes 4489344 | tf_op jit(solution)/shard_map/sdj,sij->sdi/dot_general | solution.py:16
  38.8 0.5 convolution_bitcast_fusion.2
  39.3 0.0 copy-start.3
  39.3 3.4 %fusion.4 = f32[64,6,128]{2,1,0:T(8,128)S(1)} fusion(s32[2,64,128,128]{3,2,1,0:T(8,128)} %param.15, pred[64]{0:T(512)(128)(4,1)S(1)} %iota_compare_fusion.2, bf16[64,6,128]{2,1,0:T(8,128)(2,1)S(1)} %gather_fusion.1, pred[64]{0:T(512)(128)(4,1)S(1)} %get-tuple-element.12), kind=kOutput, calls=%fused_computation.7 | convolution fusion | flops 14729216 | bytes 4489344 | tf_op jit(solution)/shard_map/sdj,sij->sdi/dot_general | solution.py:16
  42.7 0.5 convolution_bitcast_fusion.1
  43.2 0.0 copy-start.2
  43.2 0.1 pad_maximum_fusion
  43.3 1.5 %copy.31 = f32[2,128,6,128]{3,0,2,1:T(2,128)} copy(f32[2,128,6,128]{3,1,2,0:T(8,128)S(1)} %pad_maximum_fusion) | data formatting | bytes 1572864 | tf_op jit(solution)/shard_map/stack | solution.py:37
  44.7 6.4 %all-to-all-start.1 = ((f32[2,128,6,128]{3,0,2,1:T(2,128)}), f32[2,128,6,128]{3,0,2,1:T(2,128)S(1)}, u32[]{:S(2)}, u32[]{:S(2)}) async-start(f32[2,128,6,128]{3,0,2,1:T(2,128)} %copy.31), calls=%async_computation.1 | async-start | bytes 1572864 | tf_op jit(solution)/shard_map/all_to_all | solution.py:49
  51.1 0.0 copy-done.3
  51.2 21.9 %all-to-all-done.1 = f32[2,128,6,128]{3,0,2,1:T(2,128)S(1)} async-done(((f32[2,128,6,128]{3,0,2,1:T(2,128)}), f32[2,128,6,128]{3,0,2,1:T(2,128)S(1)}, u32[]{:S(2)}, u32[]{:S(2)}) %all-to-all-start.1) | async-done | bytes 786464 | tf_op jit(solution)/shard_map/all_to_all | solution.py:49
  73.1 0.0 copy-start.1
  73.1 0.3 fusion.11
  73.4 0.0 copy-done
  73.4 0.5 convolution_bitcast_fusion
  74.0 0.0 copy-done.2
  74.0 0.2 copy-done.1
  74.2 0.3 fusion.10
  74.5 9.5 %all-reduce.1 = bf16[768,128]{0,1:T(8,128)(2,1)S(1)} all-reduce(f32[768,128]{0,1:T(8,128)S(1)} %fusion.10), channel_id=1, replica_groups=mesh['feat'=128,'rel'=2] {'rel'}, use_global_device_ids=true, to_apply=%region_0.2 | all-reduce | flops 98304 | bytes 589824 | tf_op jit(solution)/shard_map/psum | solution.py:60
  84.0 0.8 copy.33
  (3 shorter events, 0.0 us)
Async XLA Ops:
  0.0 73.4 %copy-start = (bf16[2,768,768]{2,1,0:T(8,128)(2,1)S(1)}, bf16[2,768,768]{2,1,0:T(8,128)(2,1)}, u32[]{:S(2)}) copy-start(bf16[2,768,768]{2,1,0:T(8,128)(2,1)} %param.11) | copy-start | bytes 7077892
  4.5 28.3 %all-to-all-start = ((bf16[128,2,384]{2,1,0:T(2,128)(2,1)}), bf16[128,2,384]{2,1,0:T(2,128)(2,1)S(1)}, u32[]{:S(2)}, u32[]{:S(2)}) async-start(bf16[128,2,384]{2,1,0:T(2,128)(2,1)} %reshape.184), calls=%async_computation | async-start | bytes 393216 | tf_op jit(solution)/shard_map/all_to_all | solution.py:36
  39.3 11.9 %copy-start.3 = (s32[2,128]{1,0:T(2,128)S(1)}, s32[2,128]{1,0:T(2,128)}, u32[]{:S(2)}) copy-start(s32[2,128]{1,0:T(2,128)} %param.17) | copy-start | bytes 3076
  43.2 30.8 %copy-start.2 = (bf16[768,128]{1,0:T(8,128)(2,1)S(1)}, bf16[768,128]{1,0:T(8,128)(2,1)}, u32[]{:S(2)}) copy-start(bf16[768,128]{1,0:T(8,128)(2,1)} %param.10) | copy-start | bytes 589828
  44.7 28.3 %all-to-all-start.1 = ((f32[2,128,6,128]{3,0,2,1:T(2,128)}), f32[2,128,6,128]{3,0,2,1:T(2,128)S(1)}, u32[]{:S(2)}, u32[]{:S(2)}) async-start(f32[2,128,6,128]{3,0,2,1:T(2,128)} %copy.31), calls=%async_computation.1 | async-start | bytes 1572864 | tf_op jit(solution)/shard_map/all_to_all | solution.py:49
  73.1 1.1 %copy-start.1 = (bf16[384,768]{1,0:T(8,128)(2,1)S(1)}, bf16[384,768]{1,0:T(8,128)(2,1)}, u32[]{:S(2)}) copy-start(bf16[384,768]{1,0:T(8,128)(2,1)} %param.12) | copy-start | bytes 1769476
where the time goes:
time: 85.2 us; the launch traced here: 84.8 us
  waiting for transfers between devices  29.7 us (35%)
  starting transfers between devices  22.7 us (27%)
  local copies, waits for them, and re-layouts  9.88 us (12%)
  blocking collectives  9.46 us (11%)
  matrix products  8.58 us (10%)
  other arithmetic  4.25 us (5%)
    all_to_all x1, waiting for transfers between devices, shards(): lax.all_to_all(stacked, 'feat', split_axis=1, concat_axis=2, tiled=True)  21.9 us
    all_to_all x1, starting transfers between devices, shards(): lax.all_to_all(grouped, 'feat', split_axis=1, concat_axis=0, tiled=True)  16.3 us
    psum x1, blocking collectives, shards(): total_sum = lax.psum(partial_sum, 'rel')  9.46 us
    all_to_all x1, waiting for transfers between devices, shards(): lax.all_to_all(grouped, 'feat', split_axis=1, concat_axis=0, tiled=True)  7.8 us
    dot_general x2, matrix products, relation_blocks(): jnp.einsum('sdj,sij->sdi', panels, tile_group, preferred_element_type=jnp...  6.87 us
    all_to_all x1, starting transfers between devices, shards(): lax.all_to_all(stacked, 'feat', split_axis=1, concat_axis=2, tiled=True)  6.38 us
    unnamed x1, other arithmetic  1.81 us
  transfers between devices with their start and end apart: 2, of which 2 were waited for; matrix products, arithmetic and copies ran while one was open for 5% of the time, Pallas kernels for 0%

commit v1 on v0

v1 whole, which is shorter than its diff:
```python
import functools

import jax
import jax.numpy as jnp
from jax import lax
from jax.experimental import pallas as pl
from jax.experimental.pallas import tpu as pltpu
from jax.sharding import PartitionSpec as P

GROUP = 8


def spread_matrix(out_rows, in_rows, stride, take):
    out_id = lax.broadcasted_iota(jnp.int32, (out_rows, in_rows), 0)
    in_id = lax.broadcasted_iota(jnp.int32, (out_rows, in_rows), 1)
    place = out_id // stride * take + out_id % stride
    return jnp.where((out_id % stride < take) & (place == in_id), 1.0, 0.0).astype(jnp.bfloat16)


def pack_kernel(features_ref, degrees_ref, out_ref):
    take = features_ref.shape[0] // out_ref.shape[0]
    width = features_ref.shape[1]
    spread = spread_matrix(128, 16 * take, 8, take)
    degrees = degrees_ref[...].astype(jnp.float32)
    row = lax.broadcasted_iota(jnp.int32, (8, width), 0)
    tail = jnp.where(row == take, degrees[0:1], jnp.where(row == take + 1, degrees[1:2], 0.0))
    for block in range(out_ref.shape[0] // 16):
        rows = features_ref[block * 16 * take : (block + 1) * 16 * take, :]
        placed = jnp.dot(spread, rows, preferred_element_type=jnp.float32)
        out_ref[block * 16 : (block + 1) * 16] = (placed.reshape(16, 8, width) + tail[None]).astype(
            jnp.bfloat16
        )


def slots_kernel(rows_ref, cols_ref, live_ref, panels_ref, tiles_ref, out_ref, sums_ref):
    sums_ref[...] = jnp.zeros_like(sums_ref)
    relations, blocks = sums_ref.shape[0], sums_ref.shape[1]
    for relation in range(relations):
        live = live_ref[relation]

        def group(index, carry, relation=relation, live=live):
            base = index * GROUP
            parts = []
            for step in range(GROUP):
                slot = base + step
                panel = panels_ref[cols_ref[relation, slot]]
                tile = tiles_ref[relation, slot].astype(jnp.float32).astype(jnp.bfloat16)
                part = lax.dot_general(
                    panel, tile, (((1,), (1,)), ((), ())), preferred_element_type=jnp.float32
                )
                parts.append(jnp.where(slot < live, part, 0.0))
            for step in range(GROUP):
                row = rows_ref[relation, base + step]
                sums_ref[relation, row] += parts[step]
            return carry

        lax.fori_loop(0, pl.cdiv(live, GROUP), group, 0)

    def finish(index, carry):
        at = pl.ds(index * 8, 8)
        packed = panels_ref[at].astype(jnp.float32)
        take = 8 - relations
        done = [
            sums_ref[relation, at] / packed[:, take + relation : take + relation + 1, :]
            for relation in range(relations)
        ]
        out_ref[at] = jnp.concatenate(done, axis=1).astype(jnp.bfloat16)
        return carry

    lax.fori_loop(0, blocks // 8, finish, 0)


def weights_kernel(rel_ref, self_ref, features_ref, packed_ref, own_ref):
    take = rel_ref.shape[1] // 128
    relations = rel_ref.shape[0]
    rows = 16 * take
    width = 16 * 8 * relations
    out_id = lax.broadcasted_iota(jnp.int32, (rows * relations, width), 1)
    in_id = lax.broadcasted_iota(jnp.int32, (rows * relations, width), 0)
    inner = out_id % 8
    place = (out_id // 8 % relations) * rows + out_id // (8 * relations) * take + inner
    pick = jnp.where((inner < take) & (place == in_id), 1.0, 0.0).astype(jnp.bfloat16)
    for block in range(8):
        part = jnp.concatenate(
            [rel_ref[relation, block * rows : (block + 1) * rows, :] for relation in range(relations)], axis=0
        )
        packed_ref[:, block * width : (block + 1) * width] = lax.dot_general(
            part, pick, (((0,), (0,)), ((), ())), preferred_element_type=jnp.float32
        ).astype(jnp.bfloat16)
    half = self_ref.shape[0]
    start = pl.multiple_of(lax.axis_index("rel") * half, half)
    own_ref[...] = lax.dot_general(
        self_ref[...],
        features_ref[pl.ds(start, half), :],
        (((0,), (0,)), ((), ())),
        preferred_element_type=jnp.float32,
    )


def transform_kernel(packed_ref, hidden_ref, own_ref, out_ref):
    hidden = hidden_ref[...].reshape(packed_ref.shape[1], hidden_ref.shape[2])
    out_ref[...] = own_ref[...] + jnp.dot(packed_ref[...], hidden, preferred_element_type=jnp.float32)


VMEM = pl.BlockSpec(memory_space=pltpu.VMEM)
SMEM = pl.BlockSpec(memory_space=pltpu.SMEM)


def shards(
    features, rel_weight, self_weight, block_rows, block_cols, count_tiles, live_slots, degrees
):
    width_all, node_local = features.shape
    relations = rel_weight.shape[0]
    devices = 128
    send = pl.pallas_call(
        pack_kernel,
        out_shape=jax.ShapeDtypeStruct((devices, 8, node_local), jnp.bfloat16),
        in_specs=[VMEM, VMEM],
        out_specs=VMEM,
        name="pack",
    )(features, degrees)
    panels = lax.all_to_all(send, "feat", split_axis=0, concat_axis=0, tiled=True)
    packed_weight, own = pl.pallas_call(
        weights_kernel,
        out_shape=(
            jax.ShapeDtypeStruct((width_all, devices * 8 * relations), jnp.bfloat16),
            jax.ShapeDtypeStruct((width_all, node_local), jnp.float32),
        ),
        in_specs=[VMEM, VMEM, VMEM],
        out_specs=(VMEM, VMEM),
        compiler_params=pltpu.CompilerParams(vmem_limit_bytes=24 * 1024 * 1024),
        name="weights",
    )(rel_weight, self_weight, features)
    hidden = pl.pallas_call(
        slots_kernel,
        out_shape=jax.ShapeDtypeStruct((devices, 8 * relations, node_local), jnp.bfloat16),
        in_specs=[SMEM, SMEM, SMEM, VMEM, VMEM],
        out_specs=VMEM,
        scratch_shapes=[pltpu.VMEM((relations, devices, 8, node_local), jnp.float32)],
        compiler_params=pltpu.CompilerParams(vmem_limit_bytes=32 * 1024 * 1024),
        name="slots",
    )(block_rows, block_cols, live_slots, panels, count_tiles)
    gathered = lax.all_to_all(hidden, "feat", split_axis=0, concat_axis=0, tiled=True)
    partial_sum = pl.pallas_call(
        transform_kernel,
        out_shape=jax.ShapeDtypeStruct((width_all, node_local), jnp.float32),
        in_specs=[VMEM, VMEM, VMEM],
        out_specs=VMEM,
        compiler_params=pltpu.CompilerParams(vmem_limit_bytes=24 * 1024 * 1024),
        name="transform",
    )(packed_weight, gathered, own)
    other = lax.ppermute(partial_sum, "rel", [(0, 1), (1, 0)])
    return jnp.maximum(partial_sum + other, 0.0).astype(jnp.bfloat16)


def solution(mesh):
    placed = (
        P(None, "feat"),
        P("rel", None, None),
        P("rel", None),
        P("rel", None),
        P("rel", None),
        P("rel", None, None, None),
        P("rel"),
        P("rel", "feat"),
    )
    return jax.shard_map(
        shards, mesh=mesh, in_specs=placed, out_specs=P(None, "feat"), check_vma=False
    )
```

time: 85.2 us -> 75.8 us (0.89)
  blocking collectives: 9.46 us -> 29.6 us
  waiting for transfers between devices: 29.7 us -> 11.9 us
  Pallas kernels: 0 us -> 9.69 us
  starting transfers between devices: 22.7 us -> 13.3 us
  matrix products: 8.58 us -> 0 us
  other arithmetic: 4.25 us -> 0.75 us
    all_to_all x0 -> x1, blocking collectives: none -> 29.6 us  [shards(): lax.all_to_all(send, 'feat', split_axis=0, concat_axis=0, tiled=True)]
    all_to_all x2 -> x1, waiting for transfers between devices: 29.7 us -> 10.5 us  [shards(): lax.all_to_all(hidden, 'feat', split_axis=0, concat_axis=0, tiled=True)]
    all_to_all x2 -> x1, starting transfers between devices: 22.7 us -> 7.3 us  [shards(): lax.all_to_all(hidden, 'feat', split_axis=0, concat_axis=0, tiled=True)]
    pallas_call x0 -> x4, Pallas kernels: none -> 9.69 us  [the longest x1 4.57 us: shards(): pl.pallas_call(slots_kernel, out_shape=jax.ShapeDtypeStruct((devices, 8 *...]
    psum x1 -> x0, blocking collectives: 9.46 us -> none  [shards(): total_sum = lax.psum(partial_sum, 'rel')]
    dot_general x6 -> x0, matrix products: 8.58 us -> none  [the longest x2 6.87 us: relation_blocks(): jnp.einsum('sdj,sij->sdi', panels, tile_group, preferred_element_type=jnp...]
    unnamed x11 -> x18, local copies, waits for them, and re-layouts: 1.66 us -> 9.87 us
    ppermute x0 -> x1, starting transfers between devices: none -> 6.01 us  [shards(): other = lax.ppermute(partial_sum, 'rel', [(0, 1), (1, 0)])]
  transfers between devices with their start and end apart: 2 -> 2, of which waited for: 2 -> 2; matrix products, arithmetic and copies ran while one was open for 5% -> 0% of each run, Pallas kernels for 0% -> 2%
where the time goes in v1:
time: 75.8 us; the launch traced here: 75.2 us
  blocking collectives  29.6 us (39%)
  starting transfers between devices  13.3 us (18%)
  waiting for transfers between devices  11.9 us (16%)
  local copies, waits for them, and re-layouts  9.87 us (13%)
  Pallas kernels  9.69 us (13%)
    all_to_all x1, blocking collectives, shards(): lax.all_to_all(send, 'feat', split_axis=0, concat_axis=0, tiled=True)  29.6 us
    all_to_all x1, waiting for transfers between devices, shards(): lax.all_to_all(hidden, 'feat', split_axis=0, concat_axis=0, tiled=True)  10.5 us
    unnamed x18, local copies, waits for them, and re-layouts  9.87 us
    all_to_all x1, starting transfers between devices, shards(): lax.all_to_all(hidden, 'feat', split_axis=0, concat_axis=0, tiled=True)  7.3 us
    ppermute x1, starting transfers between devices, shards(): other = lax.ppermute(partial_sum, 'rel', [(0, 1), (1, 0)])  6.01 us
    pallas_call x1, Pallas kernels, shards(): pl.pallas_call(slots_kernel, out_shape=jax.ShapeDtypeStruct((devices, 8 *...  4.57 us
    pallas_call x1, Pallas kernels, shards(): pl.pallas_call(transform_kernel, out_shape=jax.ShapeDtypeStruct((width_al...  2.02 us
    pallas_call x1, Pallas kernels, shards(): pl.pallas_call(pack_kernel, out_shape=jax.ShapeDtypeStruct((devices, 8, n...  1.84 us
  transfers between devices with their start and end apart: 2, of which 2 were waited for; matrix products, arithmetic and copies ran while one was open for 0% of the time, Pallas kernels for 2%

profile of v1, /device:TPU:1, one launch (start us, length us, event | category | flops | bytes accessed | tf_op | source)
XLA Modules:
  0.0 75.2 jit_solution(14416302489265644753)
XLA Ops:
  0.0 1.8 %pack.1 = bf16[128,8,128]{2,1,0:T(8,128)(2,1)} custom-call(bf16[768,128]{1,0:T(8,128)(2,1)} %features_ref.3, s32[2,128]{1,0:T(2,128)} %degrees_ref.1), custom_call_target="tpu_custom_call" | custom-call | tf_op jit(solution)/shard_map/pack/pallas_call | solution.py:115
  1.8 29.6 %all_to_all.10.panels_ref = bf16[128,8,128]{2,1,0:T(8,128)(2,1)S(1)} all-to-all(bf16[128,8,128]{2,1,0:T(8,128)(2,1)} %pack.1), channel_id=1, replica_groups=mesh['feat'=128,'rel'=2] {'feat'}, dimensions={0} | all-to-all | bytes 524288 | tf_op jit(solution)/shard_map/all_to_all | solution.py:122
  31.5 0.0 copy-start
  31.5 3.4 %copy-done = s32[2,64,128,128]{3,2,1,0:T(8,128)S(1)} copy-done((s32[2,64,128,128]{3,2,1,0:T(8,128)S(1)}, s32[2,64,128,128]{3,2,1,0:T(8,128)}, u32[]{:S(2)}) %copy-start) | copy-done | bytes 8388632
  34.9 0.0 copy-start.6
  34.9 0.7 copy-done.6
  35.5 0.0 copy-start.7
  35.5 0.7 copy-done.7
  36.2 0.0 copy-start.8
  36.2 0.7 copy-done.8
  36.9 0.0 copy-start.2
  36.9 4.6 %slots.1 = bf16[128,16,128]{2,1,0:T(8,128)(2,1)} custom-call(s32[2,64]{1,0:T(2,128)S(1)} %copy-done.6, s32[2,64]{1,0:T(2,128)S(1)} %copy-done.7, s32[2]{0:T(128)S(1)} %copy-done.8, bf16[128,8,128]{2,1,0:T(8,128)(2,1)S(1)} %all_to_all.10.panels_ref, s32[2,64,128,128]{3,2,1,0:T(8,128)S(1)} %copy-done), custom_call_target="tpu_custom_call" | custom-call | tf_op jit(solution)/shard_map/slots/pallas_call | solution.py:134
  41.5 7.3 %all-to-all-start.1 = ((bf16[128,16,128]{2,1,0:T(8,128)(2,1)}), bf16[128,16,128]{2,1,0:T(8,128)(2,1)}, u32[]{:S(2)}, u32[]{:S(2)}) async-start(bf16[128,16,128]{2,1,0:T(8,128)(2,1)} %slots.1), calls=%async_computation.1 | async-start | bytes 1048576 | tf_op jit(solution)/shard_map/all_to_all | solution.py:143
  48.8 0.0 copy-done.2
  48.8 0.0 copy-start.1
  48.8 1.7 %copy-done.1 = bf16[2,768,768]{2,1,0:T(8,128)(2,1)S(1)} copy-done((bf16[2,768,768]{2,1,0:T(8,128)(2,1)S(1)}, bf16[2,768,768]{2,1,0:T(8,128)(2,1)}, u32[]{:S(2)}) %copy-start.1) | copy-done | bytes 2359320
  50.4 0.0 copy-start.3
  50.4 1.1 %copy-done.3 = bf16[384,768]{1,0:T(8,128)(2,1)S(1)} copy-done((bf16[384,768]{1,0:T(8,128)(2,1)S(1)}, bf16[384,768]{1,0:T(8,128)(2,1)}, u32[]{:S(2)}) %copy-start.3) | copy-done | bytes 589848
  51.5 1.3 %weights.1 = (bf16[768,2048]{1,0:T(8,128)(2,1)S(1)}, f32[768,128]{1,0:T(8,128)S(1)}) custom-call(bf16[2,768,768]{2,1,0:T(8,128)(2,1)S(1)} %copy-done.1, bf16[384,768]{1,0:T(8,128)(2,1)S(1)} %copy-done.3, bf16[768,128]{1,0:T(8,128)(2,1)S(1)} %copy-done.2), custom_call_target="tpu_custom_call" | custom-call | tf_op jit(solution)/shard_map/weights/pallas_call | solution.py:123
  52.8 0.0 copy-start.4
  52.8 0.8 %copy-done.4 = f32[768,128]{1,0:T(8,128)} copy-done((f32[768,128]{1,0:T(8,128)}, f32[768,128]{1,0:T(8,128)S(1)}, u32[]{:S(2)}) %copy-start.4) | copy-done | bytes 393240
  53.5 10.5 %all-to-all-done.1.hidden_ref = bf16[128,16,128]{2,1,0:T(8,128)(2,1)} async-done(((bf16[128,16,128]{2,1,0:T(8,128)(2,1)}), bf16[128,16,128]{2,1,0:T(8,128)(2,1)}, u32[]{:S(2)}, u32[]{:S(2)}) %all-to-all-start.1) | async-done | bytes 524320 | tf_op jit(solution)/shard_map/all_to_all | solution.py:143
  64.1 0.0 copy-start.5
  64.1 1.0 %copy-done.5 = f32[768,128]{1,0:T(8,128)S(1)} copy-done((f32[768,128]{1,0:T(8,128)S(1)}, f32[768,128]{1,0:T(8,128)}, u32[]{:S(2)}) %copy-start.5) | copy-done | bytes 393240
  65.1 2.0 %transform.1 = f32[768,128]{1,0:T(8,128)S(1)} custom-call(bf16[768,2048]{1,0:T(8,128)(2,1)S(1)} %get-tuple-element.7.packed_ref, bf16[128,16,128]{2,1,0:T(8,128)(2,1)} %all-to-all-done.1.hidden_ref, f32[768,128]{1,0:T(8,128)S(1)} %copy-done.5), custom_call_target="tpu_custom_call" | custom-call | tf_op jit(solution)/shard_map/transform/pallas_call | solution.py:144
  67.1 6.0 %collective-permute-start = (f32[768,128]{1,0:T(8,128)S(1)}, f32[768,128]{1,0:T(8,128)S(1)}, u32[]{:S(2)}, u32[]{:S(2)}) collective-permute-start(f32[768,128]{1,0:T(8,128)S(1)} %transform.1), channel_id=1, source_target_pairs={{0,1},{1,0},{2,3},{3,2},{4,5},{5,4},{6,7},{7,6},{8,9},{9,8},{10,11... | collective-permute-start | bytes 1179656 | tf_op jit(solution)/shard_map/ppermute | solution.py:152
  73.1 1.3 %collective-permute-done = f32[768,128]{1,0:T(8,128)S(1)} collective-permute-done((f32[768,128]{1,0:T(8,128)S(1)}, f32[768,128]{1,0:T(8,128)S(1)}, u32[]{:S(2)}, u32[]{:S(2)}) %collective-permute-start) | collective-permute-done | bytes 393248 | tf_op jit(solution)/shard_map/ppermute | solution.py:152
  74.4 0.7 maximum_convert_fusion
Async XLA Ops:
  31.5 3.4 %copy-start = (s32[2,64,128,128]{3,2,1,0:T(8,128)S(1)}, s32[2,64,128,128]{3,2,1,0:T(8,128)}, u32[]{:S(2)}) copy-start(s32[2,64,128,128]{3,2,1,0:T(8,128)} %tiles_ref.1) | copy-start | bytes 25165828
  34.9 0.7 copy-start.6
  35.5 0.7 copy-start.7
  36.2 0.7 copy-start.8
  36.9 11.9 %copy-start.2 = (bf16[768,128]{1,0:T(8,128)(2,1)S(1)}, bf16[768,128]{1,0:T(8,128)(2,1)}, u32[]{:S(2)}) copy-start(bf16[768,128]{1,0:T(8,128)(2,1)} %features_ref.3) | copy-start | bytes 589828
  41.5 22.6 %all-to-all-start.1 = ((bf16[128,16,128]{2,1,0:T(8,128)(2,1)}), bf16[128,16,128]{2,1,0:T(8,128)(2,1)}, u32[]{:S(2)}, u32[]{:S(2)}) async-start(bf16[128,16,128]{2,1,0:T(8,128)(2,1)} %slots.1), calls=%async_computation.1 | async-start | bytes 1048576 | tf_op jit(solution)/shard_map/all_to_all | solution.py:143
  48.8 1.7 %copy-start.1 = (bf16[2,768,768]{2,1,0:T(8,128)(2,1)S(1)}, bf16[2,768,768]{2,1,0:T(8,128)(2,1)}, u32[]{:S(2)}) copy-start(bf16[2,768,768]{2,1,0:T(8,128)(2,1)} %rel_ref.1) | copy-start | bytes 7077892
  50.4 1.1 %copy-start.3 = (bf16[384,768]{1,0:T(8,128)(2,1)S(1)}, bf16[384,768]{1,0:T(8,128)(2,1)}, u32[]{:S(2)}) copy-start(bf16[384,768]{1,0:T(8,128)(2,1)} %self_ref.1) | copy-start | bytes 1769476
  52.8 0.8 %copy-start.4 = (f32[768,128]{1,0:T(8,128)}, f32[768,128]{1,0:T(8,128)S(1)}, u32[]{:S(2)}) copy-start(f32[768,128]{1,0:T(8,128)S(1)} %get-tuple-element.8.own_ref) | copy-start | bytes 1179652
  64.1 1.0 %copy-start.5 = (f32[768,128]{1,0:T(8,128)S(1)}, f32[768,128]{1,0:T(8,128)}, u32[]{:S(2)}) copy-start(f32[768,128]{1,0:T(8,128)} %copy-done.4) | copy-start | bytes 1179652
  67.1 7.4 %collective-permute-start = (f32[768,128]{1,0:T(8,128)S(1)}, f32[768,128]{1,0:T(8,128)S(1)}, u32[]{:S(2)}, u32[]{:S(2)}) collective-permute-start(f32[768,128]{1,0:T(8,128)S(1)} %transform.1), channel_id=1, source_target_pairs={{0,1},{1,0},{2,3},{3,2},{4,5},{5,4},{6,7},{7,6},{8,9},{9,8},{10,11... | collective-permute-start | bytes 1179656 | tf_op jit(solution)/shard_map/ppermute | solution.py:152

commit v2 on v1

v2 whole, which is shorter than its diff:
```python
import functools

import jax
import jax.numpy as jnp
from jax import lax
from jax.experimental import pallas as pl
from jax.experimental.pallas import tpu as pltpu
from jax.sharding import PartitionSpec as P

GROUP = 32
CHUNK = 8
MIB = 1024 * 1024


def spread_matrix(out_rows, in_rows, stride, take):
    out_id = lax.broadcasted_iota(jnp.int32, (out_rows, in_rows), 0)
    in_id = lax.broadcasted_iota(jnp.int32, (out_rows, in_rows), 1)
    place = out_id // stride * take + out_id % stride
    return jnp.where((out_id % stride < take) & (place == in_id), 1.0, 0.0).astype(jnp.bfloat16)


def pack_kernel(features_ref, degrees_ref, out_ref):
    take = features_ref.shape[0] // out_ref.shape[0]
    width = features_ref.shape[1]
    spread = spread_matrix(128, 16 * take, 8, take)
    degrees = degrees_ref[...].astype(jnp.float32)
    row = lax.broadcasted_iota(jnp.int32, (8, width), 0)
    tail = jnp.where(row == take, degrees[0:1], jnp.where(row == take + 1, degrees[1:2], 0.0))
    for block in range(out_ref.shape[0] // 16):
        rows = features_ref[block * 16 * take : (block + 1) * 16 * take, :]
        placed = jnp.dot(spread, rows, preferred_element_type=jnp.float32)
        out_ref[block * 16 : (block + 1) * 16] = (placed.reshape(16, 8, width) + tail[None]).astype(
            jnp.bfloat16
        )


def tiles_kernel(tiles_ref, after_ref, out_ref, landing_ref, arrived_ref):
    del after_ref
    chunks, per_chunk = landing_ref.shape[0], landing_ref.shape[1]
    per_relation = tiles_ref.shape[1] // per_chunk

    def fetch(chunk):
        source = tiles_ref.at[chunk // per_relation, pl.ds(chunk % per_relation * per_chunk, per_chunk)]
        return pltpu.make_async_copy(source, landing_ref.at[chunk], arrived_ref.at[chunk])

    for chunk in range(chunks):
        fetch(chunk).start()

    def turn(chunk, carry):
        fetch(chunk).wait()
        for pair in range(per_chunk // 2):
            turned = [landing_ref[chunk, 2 * pair + side].astype(jnp.float32).T for side in range(2)]
            counts = jnp.concatenate(turned, axis=1).astype(jnp.int32).astype(jnp.int8)
            out_ref[chunk * (per_chunk // 2) + pair] = counts
        return carry

    lax.fori_loop(0, chunks, turn, 0)


def slots_kernel(rows_ref, cols_ref, live_ref, panels_ref, tiles_ref, out_ref, sums_ref):
    sums_ref[...] = jnp.zeros_like(sums_ref)
    relations, blocks, _, width = sums_ref.shape
    pairs = tiles_ref.shape[0] // relations
    for relation in range(relations):
        live = live_ref[relation]

        def group(index, carry, relation=relation, live=live):
            base = index * GROUP
            parts = []
            for step in range(0, GROUP, 2):
                slot = base + step
                panel = jnp.concatenate(
                    [panels_ref[cols_ref[relation, slot + side]] for side in range(2)], axis=0
                )
                tile = tiles_ref[relation * pairs + index * (GROUP // 2) + step // 2].astype(jnp.bfloat16)
                both = jnp.dot(panel, tile, preferred_element_type=jnp.float32)
                parts += [both[:8, :width], both[8:, width:]]
            for step in range(GROUP):
                slot = base + step
                sums_ref[relation, rows_ref[relation, slot]] += jnp.where(slot < live, parts[step], 0.0)
            return carry

        lax.fori_loop(0, pl.cdiv(live, GROUP), group, 0)

    def finish(index, carry):
        at = pl.ds(index * 8, 8)
        packed = panels_ref[at].astype(jnp.float32)
        take = 8 - relations
        done = [
            sums_ref[relation, at] / packed[:, take + relation : take + relation + 1, :]
            for relation in range(relations)
        ]
        out_ref[at] = jnp.concatenate(done, axis=1).astype(jnp.bfloat16)
        return carry

    lax.fori_loop(0, blocks // 8, finish, 0)


def weights_kernel(rel_ref, self_ref, features_ref, after_ref, turned_ref, own_ref):
    del after_ref
    depth = rel_ref.shape[1]
    for relation in range(rel_ref.shape[0]):
        for start in range(0, depth, 128):
            turned_ref[:, relation * depth + start : relation * depth + start + 128] = rel_ref[
                relation, start : start + 128, :
            ].T
    half = self_ref.shape[0]
    start = pl.multiple_of(lax.axis_index("rel") * half, half)
    own_ref[...] = lax.dot_general(
        self_ref[...],
        features_ref[pl.ds(start, half), :],
        (((0,), (0,)), ((), ())),
        preferred_element_type=jnp.float32,
    )


def transform_kernel(turned_ref, hidden_ref, own_ref, out_ref, sorted_ref):
    blocks, height, width = hidden_ref.shape
    relations = height // 8
    depth = sorted_ref.shape[0] // relations
    take = depth // blocks
    gather = 16 * take
    out_id = lax.broadcasted_iota(jnp.int32, (relations * gather, 16 * height), 0)
    in_id = lax.broadcasted_iota(jnp.int32, (relations * gather, 16 * height), 1)
    inner = out_id % gather
    place = inner // take * height + out_id // gather * 8 + inner % take
    pick = jnp.where(place == in_id, 1.0, 0.0).astype(jnp.bfloat16)
    for block in range(blocks // 16):
        rows = hidden_ref[block * 16 : (block + 1) * 16].reshape(16 * height, width)
        ordered = jnp.dot(pick, rows, preferred_element_type=jnp.float32).astype(jnp.bfloat16)
        for relation in range(relations):
            start = relation * depth + block * gather
            sorted_ref[start : start + gather, :] = ordered[relation * gather : (relation + 1) * gather]
    out_ref[...] = own_ref[...] + jnp.dot(
        turned_ref[...], sorted_ref[...], preferred_element_type=jnp.float32
    )


VMEM = pl.BlockSpec(memory_space=pltpu.VMEM)
SMEM = pl.BlockSpec(memory_space=pltpu.SMEM)
HBM = pl.BlockSpec(memory_space=pltpu.HBM)


def shards(
    features, rel_weight, self_weight, block_rows, block_cols, count_tiles, live_slots, degrees
):
    width_all, node_local = features.shape
    relations, slots, block_size, _ = count_tiles.shape
    devices = lax.axis_size("feat")
    send = pl.pallas_call(
        pack_kernel,
        out_shape=jax.ShapeDtypeStruct((devices, 8, node_local), jnp.bfloat16),
        in_specs=[VMEM, VMEM],
        out_specs=VMEM,
        compiler_params=pltpu.CompilerParams(vmem_limit_bytes=62 * MIB),
        name="pack",
    )(features, degrees)
    panels = lax.all_to_all(send, "feat", split_axis=0, concat_axis=0, tiled=True)
    chunks = relations * slots // CHUNK
    tiles = pl.pallas_call(
        tiles_kernel,
        out_shape=jax.ShapeDtypeStruct((relations * slots // 2, block_size, 2 * block_size), jnp.int8),
        in_specs=[HBM, HBM],
        out_specs=VMEM,
        scratch_shapes=[
            pltpu.VMEM((chunks, CHUNK, block_size, block_size), jnp.int32),
            pltpu.SemaphoreType.DMA((chunks,)),
        ],
        compiler_params=pltpu.CompilerParams(vmem_limit_bytes=50 * MIB),
        cost_estimate=pl.CostEstimate(flops=0, bytes_accessed=13 * MIB, transcendentals=0),
        name="tiles",
    )(count_tiles, send)
    hidden = pl.pallas_call(
        slots_kernel,
        out_shape=jax.ShapeDtypeStruct((devices, 8 * relations, node_local), jnp.bfloat16),
        in_specs=[SMEM, SMEM, SMEM, VMEM, VMEM],
        out_specs=VMEM,
        scratch_shapes=[pltpu.VMEM((relations, devices, 8, node_local), jnp.float32)],
        compiler_params=pltpu.CompilerParams(vmem_limit_bytes=8 * MIB),
        name="slots",
    )(block_rows, block_cols, live_slots, panels, tiles)
    gathered = lax.all_to_all(hidden, "feat", split_axis=0, concat_axis=0, tiled=True)
    turned_weight, own = pl.pallas_call(
        weights_kernel,
        out_shape=(
            jax.ShapeDtypeStruct((width_all, relations * width_all), jnp.bfloat16),
            jax.ShapeDtypeStruct((width_all, node_local), jnp.float32),
        ),
        in_specs=[VMEM, VMEM, VMEM, HBM],
        out_specs=(VMEM, VMEM),
        compiler_params=pltpu.CompilerParams(vmem_limit_bytes=12 * MIB),
        cost_estimate=pl.CostEstimate(flops=800_000_000, bytes_accessed=7 * MIB, transcendentals=0),
        name="weights",
    )(rel_weight, self_weight, features, hidden)
    partial_sum = pl.pallas_call(
        transform_kernel,
        out_shape=jax.ShapeDtypeStruct((width_all, node_local), jnp.float32),
        in_specs=[VMEM, VMEM, VMEM],
        out_specs=VMEM,
        scratch_shapes=[pltpu.VMEM((relations * width_all, node_local), jnp.bfloat16)],
        compiler_params=pltpu.CompilerParams(vmem_limit_bytes=8 * MIB),
        name="transform",
    )(turned_weight, gathered, own)
    other = lax.ppermute(partial_sum, "rel", [(0, 1), (1, 0)])
    return jnp.maximum(partial_sum + other, 0.0).astype(jnp.bfloat16)


def solution(mesh):
    placed = (
        P(None, "feat"),
        P("rel", None, None),
        P("rel", None),
        P("rel", None),
        P("rel", None),
        P("rel", None, None, None),
        P("rel"),
        P("rel", "feat"),
    )
    return jax.shard_map(
        shards, mesh=mesh, in_specs=placed, out_specs=P(None, "feat"), check_vma=False
    )
```

time: 75.8 us -> 65.9 us (0.87)
  blocking collectives: 29.6 us -> 0 us
  starting transfers between devices: 13.3 us -> 27.3 us
  waiting for transfers between devices: 11.9 us -> 22.6 us
  local copies, waits for them, and re-layouts: 9.87 us -> 3.72 us
  Pallas kernels: 9.69 us -> 11.3 us
    all_to_all x1 -> x0, blocking collectives: 29.6 us -> none  [shards(): lax.all_to_all(send, 'feat', split_axis=0, concat_axis=0, tiled=True)]
    all_to_all x0 -> x1, starting transfers between devices: none -> 16.3 us  [shards(): lax.all_to_all(send, 'feat', split_axis=0, concat_axis=0, tiled=True)]
    all_to_all x0 -> x1, waiting for transfers between devices: none -> 7.72 us  [shards(): lax.all_to_all(send, 'feat', split_axis=0, concat_axis=0, tiled=True)]
    unnamed x18 -> x14, local copies, waits for them, and re-layouts: 9.87 us -> 3.72 us
    pallas_call x0 -> x1, Pallas kernels: none -> 4.57 us  [shards(): pl.pallas_call(tiles_kernel, out_shape=jax.ShapeDtypeStruct((relations *...]
    all_to_all x1, waiting for transfers between devices: 10.5 us -> 13.5 us  [shards(): lax.all_to_all(hidden, 'feat', split_axis=0, concat_axis=0, tiled=True)]
    pallas_call x1, Pallas kernels: 4.57 us -> 2.88 us  [shards(): pl.pallas_call(slots_kernel, out_shape=jax.ShapeDtypeStruct((devices, 8 *...]
    ppermute x1, starting transfers between devices: 6.01 us -> 4.55 us  [shards(): other = lax.ppermute(partial_sum, 'rel', [(0, 1), (1, 0)])]
  transfers between devices with their start and end apart: 2 -> 3, of which waited for: 2 -> 3; matrix products, arithmetic and copies ran while one was open for 0% -> 0% of each run, Pallas kernels for 2% -> 8%
where the time goes in v2:
time: 65.9 us; the launch traced here: 65.7 us
  starting transfers between devices  27.3 us (41%)
  waiting for transfers between devices  22.6 us (34%)
  Pallas kernels  11.3 us (17%)
  local copies, waits for them, and re-layouts  3.72 us (6%)
  other arithmetic  0.72 us (1%)
    all_to_all x1, starting transfers between devices, shards(): lax.all_to_all(send, 'feat', split_axis=0, concat_axis=0, tiled=True)  16.3 us
    all_to_all x1, waiting for transfers between devices, shards(): lax.all_to_all(hidden, 'feat', split_axis=0, concat_axis=0, tiled=True)  13.5 us
    all_to_all x1, waiting for transfers between devices, shards(): lax.all_to_all(send, 'feat', split_axis=0, concat_axis=0, tiled=True)  7.72 us
    all_to_all x1, starting transfers between devices, shards(): lax.all_to_all(hidden, 'feat', split_axis=0, concat_axis=0, tiled=True)  6.41 us
    pallas_call x1, Pallas kernels, shards(): pl.pallas_call(tiles_kernel, out_shape=jax.ShapeDtypeStruct((relations *...  4.57 us
    ppermute x1, starting transfers between devices, shards(): other = lax.ppermute(partial_sum, 'rel', [(0, 1), (1, 0)])  4.55 us
    unnamed x14, local copies, waits for them, and re-layouts  3.72 us
    pallas_call x1, Pallas kernels, shards(): pl.pallas_call(slots_kernel, out_shape=jax.ShapeDtypeStruct((devices, 8 *...  2.88 us
  transfers between devices with their start and end apart: 3, of which 3 were waited for; matrix products, arithmetic and copies ran while one was open for 0% of the time, Pallas kernels for 8%

profile of v2, /device:TPU:1, one launch (start us, length us, event | category | flops | bytes accessed | tf_op | source)
XLA Modules:
  0.0 65.7 jit_solution(1084063639755023234)
XLA Ops:
  0.0 1.8 %pack.1.after_ref = bf16[128,8,128]{2,1,0:T(8,128)(2,1)} custom-call(bf16[768,128]{1,0:T(8,128)(2,1)} %features_ref.3, s32[2,128]{1,0:T(2,128)} %degrees_ref.1), custom_call_target="tpu_custom_call" | custom-call | tf_op jit(solution)/shard_map/pack/pallas_call | solution.py:150
  1.8 16.3 %all-to-all-start = ((bf16[128,8,128]{2,1,0:T(8,128)(2,1)}), bf16[128,8,128]{2,1,0:T(8,128)(2,1)S(1)}, u32[]{:S(2)}, u32[]{:S(2)}) async-start(bf16[128,8,128]{2,1,0:T(8,128)(2,1)} %pack.1.after_ref), calls=%async_computation | async-start | bytes 524288 | tf_op jit(solution)/shard_map/all_to_all | solution.py:158
  18.2 0.0 copy-start.1
  18.2 1.0 %copy-done.1 = bf16[128,8,128]{2,1,0:T(8,128)(2,1)S(1)} copy-done((bf16[128,8,128]{2,1,0:T(8,128)(2,1)S(1)}, bf16[128,8,128]{2,1,0:T(8,128)(2,1)}, u32[]{:S(2)}) %copy-start.1) | copy-done | bytes 262168
  19.2 0.0 copy-start.4
  19.2 0.0 copy-start.5
  19.2 0.0 copy-start.6
  19.2 4.6 %tiles.1.tiles_ref = s8[64,128,256]{2,1,0:T(32,128)(4,1)S(1)} custom-call(s32[2,64,128,128]{3,2,1,0:T(8,128)} %tiles_ref.1, bf16[128,8,128]{2,1,0:T(8,128)(2,1)S(1)} %copy-done.1), custom_call_target="tpu_custom_call" | custom-call | bytes 13631488 | tf_op jit(solution)/shard_map/tiles/pallas_call | solution.py:160
  23.8 0.0 copy-start.2
  23.8 7.7 %all-to-all-done.panels_ref = bf16[128,8,128]{2,1,0:T(8,128)(2,1)S(1)} async-done(((bf16[128,8,128]{2,1,0:T(8,128)(2,1)}), bf16[128,8,128]{2,1,0:T(8,128)(2,1)S(1)}, u32[]{:S(2)}, u32[]{:S(2)}) %all-to-all-start) | async-done | bytes 262176 | tf_op jit(solution)/shard_map/all_to_all | solution.py:158
  31.5 0.0 copy-done.4
  31.5 0.0 copy-done.5
  31.5 0.0 copy-done.6
  31.5 2.9 %slots.1.after_ref = bf16[128,16,128]{2,1,0:T(8,128)(2,1)} custom-call(s32[2,64]{1,0:T(2,128)S(1)} %copy-done.4, s32[2,64]{1,0:T(2,128)S(1)} %copy-done.5, s32[2]{0:T(128)S(1)} %copy-done.6, bf16[128,8,128]{2,1,0:T(8,128)(2,1)S(1)} %all-to-all-done.panels_ref, s8[64,128,256]{2,1,0:T(32,128)(4,1)S(1)} %tiles.1.tiles_ref), custom_call_target="tpu_custom_call" | custom-call | tf_op jit(solution)/shard_map/slots/pallas_call | solution.py:173
  34.4 6.4 %all-to-all-start.1 = ((bf16[128,16,128]{2,1,0:T(8,128)(2,1)}), bf16[128,16,128]{2,1,0:T(8,128)(2,1)S(1)}, u32[]{:S(2)}, u32[]{:S(2)}) async-start(bf16[128,16,128]{2,1,0:T(8,128)(2,1)} %slots.1.after_ref), calls=%async_computation.1 | async-start | bytes 1048576 | tf_op jit(solution)/shard_map/all_to_all | solution.py:182
  40.8 0.0 copy-done.2
  40.8 0.0 copy-start
  40.8 1.7 %copy-done = bf16[2,768,768]{2,1,0:T(8,128)(2,1)S(1)} copy-done((bf16[2,768,768]{2,1,0:T(8,128)(2,1)S(1)}, bf16[2,768,768]{2,1,0:T(8,128)(2,1)}, u32[]{:S(2)}) %copy-start) | copy-done | bytes 2359320
  42.5 0.0 copy-start.3
  42.5 1.1 %copy-done.3 = bf16[384,768]{1,0:T(8,128)(2,1)S(1)} copy-done((bf16[384,768]{1,0:T(8,128)(2,1)S(1)}, bf16[384,768]{1,0:T(8,128)(2,1)}, u32[]{:S(2)}) %copy-start.3) | copy-done | bytes 589848
  43.5 0.9 %weights.1 = (bf16[768,1536]{1,0:T(8,128)(2,1)S(1)}, f32[768,128]{1,0:T(8,128)S(1)}) custom-call(bf16[2,768,768]{2,1,0:T(8,128)(2,1)S(1)} %copy-done, bf16[384,768]{1,0:T(8,128)(2,1)S(1)} %copy-done.3, bf16[768,128]{1,0:T(8,128)(2,1)S(1)} %copy-done.2, bf16[128,16,128]{2,1,0:T(8,128)(2,1)} %slots.1.after_ref), custom_call_target="tpu_custom_call" | custom-call | flops 800000000 | bytes 7340032 | tf_op jit(solution)/shard_map/weights/pallas_call | solution.py:183
  44.4 13.5 %all-to-all-done.1.hidden_ref = bf16[128,16,128]{2,1,0:T(8,128)(2,1)S(1)} async-done(((bf16[128,16,128]{2,1,0:T(8,128)(2,1)}), bf16[128,16,128]{2,1,0:T(8,128)(2,1)S(1)}, u32[]{:S(2)}, u32[]{:S(2)}) %all-to-all-start.1) | async-done | bytes 524320 | tf_op jit(solution)/shard_map/all_to_all | solution.py:182
  57.9 1.1 %transform.1 = f32[768,128]{1,0:T(8,128)S(1)} custom-call(bf16[768,1536]{1,0:T(8,128)(2,1)S(1)} %get-tuple-element.7.turned_ref, bf16[128,16,128]{2,1,0:T(8,128)(2,1)S(1)} %all-to-all-done.1.hidden_ref, f32[768,128]{1,0:T(8,128)S(1)} %get-tuple-element.8.own_ref), custom_call_target="tpu_custom_call" | custom-call | tf_op jit(solution)/shard_map/transform/pallas_call | solution.py:195
  59.1 4.6 %collective-permute-start = (f32[768,128]{1,0:T(8,128)S(1)}, f32[768,128]{1,0:T(8,128)S(1)}, u32[]{:S(2)}, u32[]{:S(2)}) collective-permute-start(f32[768,128]{1,0:T(8,128)S(1)} %transform.1), channel_id=1, source_target_pairs={{0,1},{1,0},{2,3},{3,2},{4,5},{5,4},{6,7},{7,6},{8,9},{9,8},{10,11... | collective-permute-start | bytes 1179656 | tf_op jit(solution)/shard_map/ppermute | solution.py:204
  63.6 1.3 %collective-permute-done = f32[768,128]{1,0:T(8,128)S(1)} collective-permute-done((f32[768,128]{1,0:T(8,128)S(1)}, f32[768,128]{1,0:T(8,128)S(1)}, u32[]{:S(2)}, u32[]{:S(2)}) %collective-permute-start) | collective-permute-done | bytes 393248 | tf_op jit(solution)/shard_map/ppermute | solution.py:204
  65.0 0.7 %maximum_convert_fusion = bf16[768,128]{1,0:T(8,128)(2,1)} fusion(f32[768,128]{1,0:T(8,128)S(1)} %transform.1, f32[768,128]{1,0:T(8,128)S(1)} %collective-permute-done), kind=kLoop, calls=%fused_computation | loop fusion | flops 294912 | bytes 983040 | tf_op jit(solution)/shard_map/convert_element_type | solution.py:205
Async XLA Ops:
  1.8 29.6 %all-to-all-start = ((bf16[128,8,128]{2,1,0:T(8,128)(2,1)}), bf16[128,8,128]{2,1,0:T(8,128)(2,1)S(1)}, u32[]{:S(2)}, u32[]{:S(2)}) async-start(bf16[128,8,128]{2,1,0:T(8,128)(2,1)} %pack.1.after_ref), calls=%async_computation | async-start | bytes 524288 | tf_op jit(solution)/shard_map/all_to_all | solution.py:158
  18.2 1.0 %copy-start.1 = (bf16[128,8,128]{2,1,0:T(8,128)(2,1)S(1)}, bf16[128,8,128]{2,1,0:T(8,128)(2,1)}, u32[]{:S(2)}) copy-start(bf16[128,8,128]{2,1,0:T(8,128)(2,1)} %pack.1.after_ref) | copy-start | bytes 786436
  19.2 12.3 %copy-start.4 = (s32[2,64]{1,0:T(2,128)S(1)}, s32[2,64]{1,0:T(2,128)}, u32[]{:S(2)}) copy-start(s32[2,64]{1,0:T(2,128)} %rows_ref.1) | copy-start | bytes 1540
  19.2 12.3 %copy-start.5 = (s32[2,64]{1,0:T(2,128)S(1)}, s32[2,64]{1,0:T(2,128)}, u32[]{:S(2)}) copy-start(s32[2,64]{1,0:T(2,128)} %cols_ref.1) | copy-start | bytes 1540
  19.2 12.3 %copy-start.6 = (s32[2]{0:T(128)S(1)}, s32[2]{0:T(128)}, u32[]{:S(2)}) copy-start(s32[2]{0:T(128)} %live_ref.1) | copy-start | bytes 28
  23.8 17.0 %copy-start.2 = (bf16[768,128]{1,0:T(8,128)(2,1)S(1)}, bf16[768,128]{1,0:T(8,128)(2,1)}, u32[]{:S(2)}) copy-start(bf16[768,128]{1,0:T(8,128)(2,1)} %features_ref.3) | copy-start | bytes 589828
  34.4 23.6 %all-to-all-start.1 = ((bf16[128,16,128]{2,1,0:T(8,128)(2,1)}), bf16[128,16,128]{2,1,0:T(8,128)(2,1)S(1)}, u32[]{:S(2)}, u32[]{:S(2)}) async-start(bf16[128,16,128]{2,1,0:T(8,128)(2,1)} %slots.1.after_ref), calls=%async_computation.1 | async-start | bytes 1048576 | tf_op jit(solution)/shard_map/all_to_all | solution.py:182
  40.8 1.7 %copy-start = (bf16[2,768,768]{2,1,0:T(8,128)(2,1)S(1)}, bf16[2,768,768]{2,1,0:T(8,128)(2,1)}, u32[]{:S(2)}) copy-start(bf16[2,768,768]{2,1,0:T(8,128)(2,1)} %rel_ref.1) | copy-start | bytes 7077892
  42.5 1.1 %copy-start.3 = (bf16[384,768]{1,0:T(8,128)(2,1)S(1)}, bf16[384,768]{1,0:T(8,128)(2,1)}, u32[]{:S(2)}) copy-start(bf16[384,768]{1,0:T(8,128)(2,1)} %self_ref.1) | copy-start | bytes 1769476
  59.1 5.9 %collective-permute-start = (f32[768,128]{1,0:T(8,128)S(1)}, f32[768,128]{1,0:T(8,128)S(1)}, u32[]{:S(2)}, u32[]{:S(2)}) collective-permute-start(f32[768,128]{1,0:T(8,128)S(1)} %transform.1), channel_id=1, source_target_pairs={{0,1},{1,0},{2,3},{3,2},{4,5},{5,4},{6,7},{7,6},{8,9},{9,8},{10,11... | collective-permute-start | bytes 1179656 | tf_op jit(solution)/shard_map/ppermute | solution.py:204

commit v3 on v2

v3 whole, which is shorter than its diff:
```python
import functools

import jax
import jax.numpy as jnp
from jax import lax
from jax.experimental import pallas as pl
from jax.experimental.pallas import tpu as pltpu
from jax.sharding import PartitionSpec as P

GROUP = 32
CHUNK = 8
PARTS = 1
FIRST = 74
MIB = 1024 * 1024


def pack_kernel(features_ref, degrees_ref, out_ref):
    blocks, height, width = out_ref.shape
    take = features_ref.shape[0] // blocks
    out_id = lax.broadcasted_iota(jnp.int32, (16 * height, 16 * take), 0)
    in_id = lax.broadcasted_iota(jnp.int32, (16 * height, 16 * take), 1)
    inner = out_id % height
    place = out_id // height * take + inner
    spread = jnp.where((inner < take) & (place == in_id), 1.0, 0.0).astype(jnp.bfloat16)
    row = lax.broadcasted_iota(jnp.int32, (height, width), 0)
    degrees = degrees_ref[...].astype(jnp.float32)
    tail = jnp.where(row == take, degrees[0:1], jnp.where(row == take + 1, degrees[1:2], 0.0))
    for start in range(0, blocks, 16):
        rows = features_ref[start * take : (start + 16) * take, :]
        placed = jnp.dot(spread, rows, preferred_element_type=jnp.float32).reshape(16, height, width)
        out_ref[start : start + 16] = (placed + tail[None]).astype(jnp.bfloat16)


def tiles_kernel(tiles_ref, self_ref, features_ref, out_ref, own_ref, landing_ref, arrived_ref):
    chunks, per_chunk = landing_ref.shape[0], landing_ref.shape[1]
    per_relation = tiles_ref.shape[1] // per_chunk

    def fetch(chunk):
        source = tiles_ref.at[chunk // per_relation, pl.ds(chunk % per_relation * per_chunk, per_chunk)]
        return pltpu.make_async_copy(source, landing_ref.at[chunk], arrived_ref.at[chunk])

    for chunk in range(chunks):
        fetch(chunk).start()
    half = self_ref.shape[0]
    start = pl.multiple_of(lax.axis_index("rel") * half, half)
    own_ref[...] = lax.dot_general(
        self_ref[...],
        features_ref[pl.ds(start, half), :],
        (((0,), (0,)), ((), ())),
        preferred_element_type=jnp.float32,
    )

    def turn(chunk, carry):
        fetch(chunk).wait()
        for pair in range(per_chunk // 2):
            turned = [landing_ref[chunk, 2 * pair + side].astype(jnp.float32).T for side in range(2)]
            counts = jnp.concatenate(turned, axis=1).astype(jnp.int32).astype(jnp.int8)
            out_ref[chunk * (per_chunk // 2) + pair] = counts
        return carry

    lax.fori_loop(0, chunks, turn, 0)


def slots_kernel(
    rows_hbm, cols_hbm, live_hbm, panels_ref, tiles_ref, out_ref, token_ref,
    rows_ref, cols_ref, live_ref, sums_ref, done_ref, in_sem, out_sem,
):
    pulls = [
        pltpu.make_async_copy(source, target, in_sem.at[index])
        for index, (source, target) in enumerate(
            ((rows_hbm, rows_ref), (cols_hbm, cols_ref), (live_hbm, live_ref))
        )
    ]
    for pull in pulls:
        pull.start()
    token_ref[...] = jnp.zeros_like(token_ref)
    sums_ref[...] = jnp.zeros_like(sums_ref)
    for pull in pulls:
        pull.wait()
    relations, blocks, height, width = sums_ref.shape
    take = height - relations
    pairs = tiles_ref.shape[0] // relations

    def position(block):
        return jnp.bitwise_xor(block, FIRST)

    def add_group(relation, base, live):
        parts = []
        for step in range(0, GROUP, 2):
            slot = base + step
            panel = jnp.concatenate(
                [panels_ref[position(cols_ref[relation, slot + side])] for side in range(2)], axis=0
            )
            tile = tiles_ref[relation * pairs + slot // 2].astype(jnp.bfloat16)
            both = jnp.dot(panel, tile, preferred_element_type=jnp.float32)
            parts += [both[:height, :width], both[height:, width:]]
        for step in range(GROUP):
            slot = base + step
            part = parts[step] if live is None else jnp.where(slot < live, parts[step], 0.0)
            sums_ref[relation, position(rows_ref[relation, slot])] += part

    for relation in range(relations):
        add_group(relation, 0, None)
    for relation in range(relations):
        live = live_ref[relation]
        for base in range(GROUP, rows_ref.shape[1], GROUP):
            pl.when(live > base)(functools.partial(add_group, relation, base, live))

    part_blocks = blocks // PARTS

    def store(part):
        at = pl.ds(part * part_blocks, part_blocks)
        return pltpu.make_async_copy(done_ref.at[at], out_ref.at[at], out_sem.at[part])

    for part in range(PARTS):

        def finish(index, carry, part=part):
            at = pl.ds(part * part_blocks + index * 8, 8)
            packed = panels_ref[at].astype(jnp.float32)
            first, second = [
                sums_ref[relation, at] / packed[:, take + relation : take + relation + 1, :]
                for relation in range(2)
            ]
            rest = jnp.concatenate([first[:, 4:6], second[:, 4:6]], axis=1)
            done_ref[at, :, 0:width] = first[:, 0:4].astype(jnp.bfloat16)
            done_ref[at, :, width : 2 * width] = second[:, 0:4].astype(jnp.bfloat16)
            done_ref[at, :, 2 * width : 3 * width] = rest.astype(jnp.bfloat16)
            return carry

        lax.fori_loop(0, part_blocks // 8, finish, 0)
        store(part).start()
    for part in range(PARTS):
        store(part).wait()


def weights_kernel(rel_ref, token_ref, turned_ref):
    del token_ref
    depth = rel_ref.shape[1]
    for relation in range(rel_ref.shape[0]):
        for start in range(0, depth, 128):
            turned_ref[:, relation * depth + start : relation * depth + start + 128] = rel_ref[
                relation, start : start + 128, :
            ].T


def transform_kernel(turned_ref, hidden_ref, own_ref, out_ref, sorted_ref):
    blocks = hidden_ref.shape[0]
    width = sorted_ref.shape[1]
    depth = sorted_ref.shape[0] // 2
    take = depth // blocks
    gather = 16 * take
    out_id = lax.broadcasted_iota(jnp.int32, (2 * gather, 2 * gather), 0)
    in_id = lax.broadcasted_iota(jnp.int32, (2 * gather, 2 * gather), 1)
    relation_id = out_id // gather
    source = out_id % gather // take
    inner = out_id % take
    place = jnp.where(
        inner < 4,
        relation_id * 64 + source * 4 + inner,
        128 + source * 4 + relation_id * 2 + inner - 4,
    )
    pick = jnp.where(place == in_id, 1.0, 0.0).astype(jnp.bfloat16)
    for block in range(blocks // 16):
        at = slice(block * 16, (block + 1) * 16)
        rows = jnp.concatenate(
            [hidden_ref[at, :, lane * width : (lane + 1) * width].reshape(64, width) for lane in range(3)],
            axis=0,
        )
        ordered = jnp.dot(pick, rows, preferred_element_type=jnp.float32).astype(jnp.bfloat16)
        for relation in range(2):
            start = relation * depth + block * gather
            sorted_ref[start : start + gather, :] = ordered[relation * gather : (relation + 1) * gather]
    out_ref[...] = own_ref[...] + jnp.dot(
        turned_ref[...], sorted_ref[...], preferred_element_type=jnp.float32
    )


VMEM = pl.BlockSpec(memory_space=pltpu.VMEM)
ANY = pl.BlockSpec(memory_space=pl.ANY)
DMA = pltpu.SemaphoreType.DMA
TOKEN = jax.ShapeDtypeStruct((8, 128), jnp.float32)


def vmem_params(mib):
    return pltpu.CompilerParams(vmem_limit_bytes=mib * MIB)


def shards(
    features, rel_weight, self_weight, block_rows, block_cols, count_tiles, live_slots, degrees
):
    width_all, width = features.shape
    relations, slots, block_size, _ = count_tiles.shape
    blocks = lax.axis_size("feat")
    height = width_all // blocks + relations
    send = pl.pallas_call(
        pack_kernel,
        out_shape=jax.ShapeDtypeStruct((blocks, height, width), jnp.bfloat16),
        in_specs=[VMEM, VMEM],
        out_specs=VMEM,
        compiler_params=vmem_params(62),
        name="pack",
    )(features, degrees)
    order = [[FIRST ^ index for index in range(blocks)]]
    panels = lax.all_to_all(
        send, "feat", split_axis=0, concat_axis=0, tiled=True, axis_index_groups=order
    )
    chunks = relations * slots // CHUNK
    tiles, own = pl.pallas_call(
        tiles_kernel,
        out_shape=(
            jax.ShapeDtypeStruct((relations * slots // 2, block_size, 2 * block_size), jnp.int8),
            jax.ShapeDtypeStruct((width_all, width), jnp.float32),
        ),
        in_specs=[ANY, VMEM, VMEM],
        out_specs=(VMEM, VMEM),
        scratch_shapes=[
            pltpu.VMEM((chunks, CHUNK, block_size, block_size), jnp.int32),
            DMA((chunks,)),
        ],
        compiler_params=vmem_params(50),
        cost_estimate=pl.CostEstimate(flops=100_000_000, bytes_accessed=13 * MIB, transcendentals=0),
        name="tiles",
    )(count_tiles, self_weight, features)
    hidden, token = pl.pallas_call(
        slots_kernel,
        out_shape=(jax.ShapeDtypeStruct((blocks, 4, 3 * width), jnp.bfloat16), TOKEN),
        in_specs=[ANY, ANY, ANY, VMEM, VMEM],
        out_specs=(ANY, VMEM),
        scratch_shapes=[
            pltpu.SMEM(block_rows.shape, jnp.int32),
            pltpu.SMEM(block_cols.shape, jnp.int32),
            pltpu.SMEM(live_slots.shape, jnp.int32),
            pltpu.VMEM((relations, blocks, height, width), jnp.float32),
            pltpu.VMEM((blocks, 4, 3 * width), jnp.bfloat16),
            DMA((3,)),
            DMA((PARTS,)),
        ],
        compiler_params=vmem_params(8),
        name="slots",
    )(block_rows, block_cols, live_slots, panels, tiles)
    gathered = lax.all_to_all(
        hidden, "feat", split_axis=0, concat_axis=0, tiled=True, axis_index_groups=order
    )
    turned_weight = pl.pallas_call(
        weights_kernel,
        out_shape=jax.ShapeDtypeStruct((width_all, relations * width_all), jnp.bfloat16),
        in_specs=[VMEM, ANY],
        out_specs=VMEM,
        compiler_params=vmem_params(12),
        cost_estimate=pl.CostEstimate(flops=0, bytes_accessed=5 * MIB, transcendentals=0),
        name="weights",
    )(rel_weight, token)
    partial_sum = pl.pallas_call(
        transform_kernel,
        out_shape=jax.ShapeDtypeStruct((width_all, width), jnp.float32),
        in_specs=[VMEM, VMEM, VMEM],
        out_specs=VMEM,
        scratch_shapes=[pltpu.VMEM((relations * width_all, width), jnp.bfloat16)],
        compiler_params=vmem_params(8),
        name="transform",
    )(turned_weight, gathered, own)
    other = lax.ppermute(partial_sum, "rel", [(0, 1), (1, 0)])
    return jnp.maximum(partial_sum + other, 0.0).astype(jnp.bfloat16)


def solution(mesh):
    placed = (
        P(None, "feat"),
        P("rel", None, None),
        P("rel", None),
        P("rel", None),
        P("rel", None),
        P("rel", None, None, None),
        P("rel"),
        P("rel", "feat"),
    )
    return jax.shard_map(
        shards, mesh=mesh, in_specs=placed, out_specs=P(None, "feat"), check_vma=False
    )
```

time: 65.9 us -> 56.5 us (0.86)
  waiting for transfers between devices: 22.6 us -> 7.05 us
  starting transfers between devices: 27.3 us -> 33.8 us
    all_to_all x2, waiting for transfers between devices: 21.3 us -> 5.7 us  [the longest x1 5.7 us: shards(): lax.all_to_all(hidden, 'feat', split_axis=0, concat_axis=0, tiled=True, a...]
    all_to_all x2, starting transfers between devices: 22.7 us -> 32 us  [the longest x1 18.8 us: shards(): lax.all_to_all(send, 'feat', split_axis=0, concat_axis=0, tiled=True, axi...]
    ppermute x1, starting transfers between devices: 4.55 us -> 1.77 us  [shards(): other = lax.ppermute(partial_sum, 'rel', [(0, 1), (1, 0)])]
    unnamed x14 -> x12, local copies, waits for them, and re-layouts: 3.72 us -> 3.66 us
  transfers between devices with their start and end apart: 3 -> 3, of which waited for: 3 -> 2; matrix products, arithmetic and copies ran while one was open for 0% -> 0% of each run, Pallas kernels for 8% -> 9%
where the time goes in v3:
time: 56.5 us; the launch traced here: 56.3 us
  starting transfers between devices  33.8 us (60%)
  Pallas kernels  11 us (19%)
  waiting for transfers between devices  7.05 us (12%)
  local copies, waits for them, and re-layouts  3.66 us (6%)
  other arithmetic  0.72 us (1%)
    all_to_all x1, starting transfers between devices, shards(): lax.all_to_all(send, 'feat', split_axis=0, concat_axis=0, tiled=True, axi...  18.8 us
    all_to_all x1, starting transfers between devices, shards(): lax.all_to_all(hidden, 'feat', split_axis=0, concat_axis=0, tiled=True, a...  13.2 us
    all_to_all x1, waiting for transfers between devices, shards(): lax.all_to_all(hidden, 'feat', split_axis=0, concat_axis=0, tiled=True, a...  5.7 us
    pallas_call x1, Pallas kernels, shards(): pl.pallas_call(tiles_kernel, out_shape=(jax.ShapeDtypeStruct((relations *...  4.57 us
    unnamed x12, local copies, waits for them, and re-layouts  3.66 us
    pallas_call x1, Pallas kernels, shards(): pl.pallas_call(slots_kernel, out_shape=(jax.ShapeDtypeStruct((blocks, 4,...  2.69 us
    pallas_call x1, Pallas kernels, shards(): pl.pallas_call(pack_kernel, out_shape=jax.ShapeDtypeStruct((blocks, heigh...  1.84 us
    ppermute x1, starting transfers between devices, shards(): other = lax.ppermute(partial_sum, 'rel', [(0, 1), (1, 0)])  1.77 us
  transfers between devices with their start and end apart: 3, of which 2 were waited for; matrix products, arithmetic and copies ran while one was open for 0% of the time, Pallas kernels for 9%

profile of v3, /device:TPU:1, one launch (start us, length us, event | category | flops | bytes accessed | tf_op | source)
XLA Modules:
  0.0 56.3 jit_solution(3550126495108889494)
XLA Ops:
  0.0 1.8 %pack.1 = bf16[128,8,128]{2,1,0:T(8,128)(2,1)} custom-call(bf16[768,128]{1,0:T(8,128)(2,1)} %features_ref.3, s32[2,128]{1,0:T(2,128)} %degrees_ref.1), custom_call_target="tpu_custom_call" | custom-call | tf_op jit(solution)/shard_map/pack/pallas_call | solution.py:195
  1.8 18.8 %all-to-all-start = ((bf16[128,8,128]{2,1,0:T(8,128)(2,1)}), bf16[128,8,128]{2,1,0:T(8,128)(2,1)S(1)}, u32[]{:S(2)}, u32[]{:S(2)}) async-start(bf16[128,8,128]{2,1,0:T(8,128)(2,1)} %pack.1), calls=%async_computation | async-start | bytes 524288 | tf_op jit(solution)/shard_map/all_to_all | solution.py:204
  20.7 0.0 copy-start.1
  20.7 0.9 %copy-done.1 = bf16[768,128]{1,0:T(8,128)(2,1)S(1)} copy-done((bf16[768,128]{1,0:T(8,128)(2,1)S(1)}, bf16[768,128]{1,0:T(8,128)(2,1)}, u32[]{:S(2)}) %copy-start.1) | copy-done | bytes 196632
  21.6 0.0 copy-start.2
  21.6 1.1 %copy-done.2 = bf16[384,768]{1,0:T(8,128)(2,1)S(1)} copy-done((bf16[384,768]{1,0:T(8,128)(2,1)S(1)}, bf16[384,768]{1,0:T(8,128)(2,1)}, u32[]{:S(2)}) %copy-start.2) | copy-done | bytes 589848
  22.7 0.0 copy-start.3
  22.7 0.0 copy-start.4
  22.7 0.0 copy-start.5
  22.7 4.6 %tiles.1 = (s8[64,128,256]{2,1,0:T(32,128)(4,1)S(1)}, f32[768,128]{1,0:T(8,128)S(1)}) custom-call(s32[2,64,128,128]{3,2,1,0:T(8,128)} %tiles_ref.1, bf16[384,768]{1,0:T(8,128)(2,1)S(1)} %copy-done.2, bf16[768,128]{1,0:T(8,128)(2,1)S(1)} %copy-done.1), custom_call_target="tpu_custom_call" | custom-call | flops 100000000 | bytes 13631488 | tf_op jit(solution)/shard_map/tiles/pallas_call | solution.py:208
  27.3 0.0 all-to-all-done.panels_ref
  27.3 0.0 copy-done.3
  27.3 0.0 copy-done.4
  27.3 0.0 copy-done.5
  27.3 2.7 %slots.1 = (bf16[128,4,384]{2,1,0:T(4,128)(2,1)}, f32[8,128]{1,0:T(8,128)S(1)}) custom-call(s32[2,64]{1,0:T(2,128)S(1)} %copy-done.3, s32[2,64]{1,0:T(2,128)S(1)} %copy-done.4, s32[2]{0:T(128)S(1)} %copy-done.5, bf16[128,8,128]{2,1,0:T(8,128)(2,1)S(1)} %all-to-all-done.panels_ref, s8[64,128,256]{2,1,0:T(32,128)(4,1)S(1)} %get-tuple-element.9.tiles_ref), custom_call_target="tpu_custom_call" | custom-call | tf_op jit(solution)/shard_map/slots/pallas_call | solution.py:224
  30.0 13.2 %all-to-all-start.1 = ((bf16[128,4,384]{2,1,0:T(4,128)(2,1)}), bf16[128,4,384]{2,1,0:T(4,128)(2,1)S(1)}, u32[]{:S(2)}, u32[]{:S(2)}) async-start(bf16[128,4,384]{2,1,0:T(4,128)(2,1)} %get-tuple-element.11), calls=%async_computation.1 | async-start | bytes 786432 | tf_op jit(solution)/shard_map/all_to_all | solution.py:241
  43.2 0.0 copy-start
  43.2 1.7 %copy-done = bf16[2,768,768]{2,1,0:T(8,128)(2,1)S(1)} copy-done((bf16[2,768,768]{2,1,0:T(8,128)(2,1)S(1)}, bf16[2,768,768]{2,1,0:T(8,128)(2,1)}, u32[]{:S(2)}) %copy-start) | copy-done | bytes 2359320
  44.9 0.7 %weights.1.turned_ref = bf16[768,1536]{1,0:T(8,128)(2,1)S(1)} custom-call(bf16[2,768,768]{2,1,0:T(8,128)(2,1)S(1)} %copy-done, f32[8,128]{1,0:T(8,128)S(1)} %get-tuple-element.10.token_ref), custom_call_target="tpu_custom_call" | custom-call | bytes 5242880 | tf_op jit(solution)/shard_map/weights/pallas_call | solution.py:244
  45.5 5.7 %all-to-all-done.1.hidden_ref = bf16[128,4,384]{2,1,0:T(4,128)(2,1)S(1)} async-done(((bf16[128,4,384]{2,1,0:T(4,128)(2,1)}), bf16[128,4,384]{2,1,0:T(4,128)(2,1)S(1)}, u32[]{:S(2)}, u32[]{:S(2)}) %all-to-all-start.1) | async-done | bytes 393248 | tf_op jit(solution)/shard_map/all_to_all | solution.py:241
  51.2 1.2 %transform.1 = f32[768,128]{1,0:T(8,128)S(1)} custom-call(bf16[768,1536]{1,0:T(8,128)(2,1)S(1)} %weights.1.turned_ref, bf16[128,4,384]{2,1,0:T(4,128)(2,1)S(1)} %all-to-all-done.1.hidden_ref, f32[768,128]{1,0:T(8,128)S(1)} %get-tuple-element.12.own_ref), custom_call_target="tpu_custom_call" | custom-call | tf_op jit(solution)/shard_map/transform/pallas_call | solution.py:253
  52.5 1.8 %collective-permute-start = (f32[768,128]{1,0:T(8,128)S(1)}, f32[768,128]{1,0:T(8,128)S(1)}, u32[]{:S(2)}, u32[]{:S(2)}) collective-permute-start(f32[768,128]{1,0:T(8,128)S(1)} %transform.1), channel_id=1, source_target_pairs={{0,1},{1,0},{2,3},{3,2},{4,5},{5,4},{6,7},{7,6},{8,9},{9,8},{10,11... | collective-permute-start | bytes 1179656 | tf_op jit(solution)/shard_map/ppermute | solution.py:262
  54.2 1.3 %collective-permute-done = f32[768,128]{1,0:T(8,128)S(1)} collective-permute-done((f32[768,128]{1,0:T(8,128)S(1)}, f32[768,128]{1,0:T(8,128)S(1)}, u32[]{:S(2)}, u32[]{:S(2)}) %collective-permute-start) | collective-permute-done | bytes 393248 | tf_op jit(solution)/shard_map/ppermute | solution.py:262
  55.6 0.7 %maximum_convert_fusion = bf16[768,128]{1,0:T(8,128)(2,1)} fusion(f32[768,128]{1,0:T(8,128)S(1)} %transform.1, f32[768,128]{1,0:T(8,128)S(1)} %collective-permute-done), kind=kLoop, calls=%fused_computation | loop fusion | flops 294912 | bytes 983040 | tf_op jit(solution)/shard_map/convert_element_type | solution.py:263
Async XLA Ops:
  1.8 25.4 %all-to-all-start = ((bf16[128,8,128]{2,1,0:T(8,128)(2,1)}), bf16[128,8,128]{2,1,0:T(8,128)(2,1)S(1)}, u32[]{:S(2)}, u32[]{:S(2)}) async-start(bf16[128,8,128]{2,1,0:T(8,128)(2,1)} %pack.1), calls=%async_computation | async-start | bytes 524288 | tf_op jit(solution)/shard_map/all_to_all | solution.py:204
  20.7 0.9 %copy-start.1 = (bf16[768,128]{1,0:T(8,128)(2,1)S(1)}, bf16[768,128]{1,0:T(8,128)(2,1)}, u32[]{:S(2)}) copy-start(bf16[768,128]{1,0:T(8,128)(2,1)} %features_ref.3) | copy-start | bytes 589828
  21.6 1.1 %copy-start.2 = (bf16[384,768]{1,0:T(8,128)(2,1)S(1)}, bf16[384,768]{1,0:T(8,128)(2,1)}, u32[]{:S(2)}) copy-start(bf16[384,768]{1,0:T(8,128)(2,1)} %self_ref.1) | copy-start | bytes 1769476
  22.7 4.6 %copy-start.3 = (s32[2,64]{1,0:T(2,128)S(1)}, s32[2,64]{1,0:T(2,128)}, u32[]{:S(2)}) copy-start(s32[2,64]{1,0:T(2,128)} %rows_hbm.1) | copy-start | bytes 1540
  22.7 4.6 %copy-start.4 = (s32[2,64]{1,0:T(2,128)S(1)}, s32[2,64]{1,0:T(2,128)}, u32[]{:S(2)}) copy-start(s32[2,64]{1,0:T(2,128)} %cols_hbm.1) | copy-start | bytes 1540
  22.7 4.6 %copy-start.5 = (s32[2]{0:T(128)S(1)}, s32[2]{0:T(128)}, u32[]{:S(2)}) copy-start(s32[2]{0:T(128)} %live_hbm.1) | copy-start | bytes 28
  30.0 21.2 %all-to-all-start.1 = ((bf16[128,4,384]{2,1,0:T(4,128)(2,1)}), bf16[128,4,384]{2,1,0:T(4,128)(2,1)S(1)}, u32[]{:S(2)}, u32[]{:S(2)}) async-start(bf16[128,4,384]{2,1,0:T(4,128)(2,1)} %get-tuple-element.11), calls=%async_computation.1 | async-start | bytes 786432 | tf_op jit(solution)/shard_map/all_to_all | solution.py:241
  43.2 1.7 %copy-start = (bf16[2,768,768]{2,1,0:T(8,128)(2,1)S(1)}, bf16[2,768,768]{2,1,0:T(8,128)(2,1)}, u32[]{:S(2)}) copy-start(bf16[2,768,768]{2,1,0:T(8,128)(2,1)} %rel_ref.1) | copy-start | bytes 7077892
  52.5 3.1 %collective-permute-start = (f32[768,128]{1,0:T(8,128)S(1)}, f32[768,128]{1,0:T(8,128)S(1)}, u32[]{:S(2)}, u32[]{:S(2)}) collective-permute-start(f32[768,128]{1,0:T(8,128)S(1)} %transform.1), channel_id=1, source_target_pairs={{0,1},{1,0},{2,3},{3,2},{4,5},{5,4},{6,7},{7,6},{8,9},{9,8},{10,11... | collective-permute-start | bytes 1179656 | tf_op jit(solution)/shard_map/ppermute | solution.py:262

commit v4 on v3

--- a/solution.py
+++ b/solution.py
@@ -11,6 +11,7 @@
 CHUNK = 8
 PARTS = 1
 FIRST = 74
+PADDED_PAIRS = 80
 MIB = 1024 * 1024
 
 
@@ -31,7 +32,7 @@
         out_ref[start : start + 16] = (placed + tail[None]).astype(jnp.bfloat16)
 
 
-def tiles_kernel(tiles_ref, self_ref, features_ref, out_ref, own_ref, landing_ref, arrived_ref):
+def tiles_kernel(tiles_ref, out_ref, landing_ref, arrived_ref):
     chunks, per_chunk = landing_ref.shape[0], landing_ref.shape[1]
     per_relation = tiles_ref.shape[1] // per_chunk
 
@@ -41,14 +42,6 @@
 
     for chunk in range(chunks):
         fetch(chunk).start()
-    half = self_ref.shape[0]
-    start = pl.multiple_of(lax.axis_index("rel") * half, half)
-    own_ref[...] = lax.dot_general(
-        self_ref[...],
-        features_ref[pl.ds(start, half), :],
-        (((0,), (0,)), ((), ())),
-        preferred_element_type=jnp.float32,
-    )
 
     def turn(chunk, carry):
         fetch(chunk).wait()
@@ -79,7 +72,7 @@
         pull.wait()
     relations, blocks, height, width = sums_ref.shape
     take = height - relations
-    pairs = tiles_ref.shape[0] // relations
+    pairs = rows_ref.shape[1] // 2
 
     def position(block):
         return jnp.bitwise_xor(block, FIRST)
@@ -133,46 +126,45 @@
         store(part).wait()
 
 
-def weights_kernel(rel_ref, token_ref, turned_ref):
+def weights_kernel(rel_ref, self_ref, features_ref, token_ref, turned_ref, own_ref):
     del token_ref
     depth = rel_ref.shape[1]
-    for relation in range(rel_ref.shape[0]):
-        for start in range(0, depth, 128):
-            turned_ref[:, relation * depth + start : relation * depth + start + 128] = rel_ref[
-                relation, start : start + 128, :
-            ].T
-
-
-def transform_kernel(turned_ref, hidden_ref, own_ref, out_ref, sorted_ref):
+    take = depth // 128
+    gather = 16 * take
+    row = lax.broadcasted_iota(jnp.int32, (2 * gather, 2 * gather), 0)
+    column = lax.broadcasted_iota(jnp.int32, (2 * gather, 2 * gather), 1)
+    third, source, inner = column // 64, column % 64 // 4, column % 4
+    relation_id = jnp.where(third < 2, third, inner // 2)
+    feature = source * take + jnp.where(third < 2, inner, 4 + inner % 2)
+    pick = jnp.where(relation_id * gather + feature == row, 1.0, 0.0).astype(jnp.bfloat16)
+    for block in range(8):
+        rows = jnp.concatenate(
+            [rel_ref[relation, block * gather : (block + 1) * gather, :] for relation in range(2)], axis=0
+        )
+        moved = lax.dot_general(
+            rows, pick, (((0,), (0,)), ((), ())), preferred_element_type=jnp.float32
+        ).astype(jnp.bfloat16)
+        for lane in range(3):
+            start = lane * (2 * depth // 3) + block * 64
+            turned_ref[:, start : start + 64] = moved[:, lane * 64 : (lane + 1) * 64]
+    half = self_ref.shape[0]
+    start = pl.multiple_of(lax.axis_index("rel") * half, half)
+    own_ref[...] = lax.dot_general(
+        self_ref[...],
+        features_ref[pl.ds(start, half), :],
+        (((0,), (0,)), ((), ())),
+        preferred_element_type=jnp.float32,
+    )
+
+
+def transform_kernel(turned_ref, hidden_ref, own_ref, out_ref):
     blocks = hidden_ref.shape[0]
-    width = sorted_ref.shape[1]
-    depth = sorted_ref.shape[0] // 2
-    take = depth // blocks
-    gather = 16 * take
-    out_id = lax.broadcasted_iota(jnp.int32, (2 * gather, 2 * gather), 0)
-    in_id = lax.broadcasted_iota(jnp.int32, (2 * gather, 2 * gather), 1)
-    relation_id = out_id // gather
-    source = out_id % gather // take
-    inner = out_id % take
-    place = jnp.where(
-        inner < 4,
-        relation_id * 64 + source * 4 + inner,
-        128 + source * 4 + relation_id * 2 + inner - 4,
-    )
-    pick = jnp.where(place == in_id, 1.0, 0.0).astype(jnp.bfloat16)
-    for block in range(blocks // 16):
-        at = slice(block * 16, (block + 1) * 16)
-        rows = jnp.concatenate(
-            [hidden_ref[at, :, lane * width : (lane + 1) * width].reshape(64, width) for lane in range(3)],
-            axis=0,
-        )
-        ordered = jnp.dot(pick, rows, preferred_element_type=jnp.float32).astype(jnp.bfloat16)
-        for relation in range(2):
-            start = relation * depth + block * gather
-            sorted_ref[start : start + gather, :] = ordered[relation * gather : (relation + 1) * gather]
-    out_ref[...] = own_ref[...] + jnp.dot(
-        turned_ref[...], sorted_ref[...], preferred_element_type=jnp.float32
-    )
+    width = own_ref.shape[1]
+    hidden = jnp.concatenate(
+        [hidden_ref[:, :, lane * width : (lane + 1) * width].reshape(4 * blocks, width) for lane in range(3)],
+        axis=0,
+    )
+    out_ref[...] = own_ref[...] + jnp.dot(turned_ref[...], hidden, preferred_element_type=jnp.float32)
 
 
 VMEM = pl.BlockSpec(memory_space=pltpu.VMEM)
@@ -205,22 +197,19 @@
         send, "feat", split_axis=0, concat_axis=0, tiled=True, axis_index_groups=order
     )
     chunks = relations * slots // CHUNK
-    tiles, own = pl.pallas_call(
+    tiles = pl.pallas_call(
         tiles_kernel,
-        out_shape=(
-            jax.ShapeDtypeStruct((relations * slots // 2, block_size, 2 * block_size), jnp.int8),
-            jax.ShapeDtypeStruct((width_all, width), jnp.float32),
-        ),
-        in_specs=[ANY, VMEM, VMEM],
-        out_specs=(VMEM, VMEM),
+        out_shape=jax.ShapeDtypeStruct((PADDED_PAIRS, block_size, 2 * block_size), jnp.int8),
+        in_specs=[ANY],
+        out_specs=VMEM,
         scratch_shapes=[
             pltpu.VMEM((chunks, CHUNK, block_size, block_size), jnp.int32),
             DMA((chunks,)),
         ],
         compiler_params=vmem_params(50),
-        cost_estimate=pl.CostEstimate(flops=100_000_000, bytes_accessed=13 * MIB, transcendentals=0),
+        cost_estimate=pl.CostEstimate(flops=0, bytes_accessed=13 * MIB, transcendentals=0),
         name="tiles",
-    )(count_tiles, self_weight, features)
+    )(count_tiles)
     hidden, token = pl.pallas_call(
         slots_kernel,
         out_shape=(jax.ShapeDtypeStruct((blocks, 4, 3 * width), jnp.bfloat16), TOKEN),
@@ -241,21 +230,23 @@
     gathered = lax.all_to_all(
         hidden, "feat", split_axis=0, concat_axis=0, tiled=True, axis_index_groups=order
     )
-    turned_weight = pl.pallas_call(
+    turned_weight, own = pl.pallas_call(
         weights_kernel,
-        out_shape=jax.ShapeDtypeStruct((width_all, relations * width_all), jnp.bfloat16),
-        in_specs=[VMEM, ANY],
-        out_specs=VMEM,
+        out_shape=(
+            jax.ShapeDtypeStruct((width_all, relations * width_all), jnp.bfloat16),
+            jax.ShapeDtypeStruct((width_all, width), jnp.float32),
+        ),
+        in_specs=[VMEM, VMEM, VMEM, ANY],
+        out_specs=(VMEM, VMEM),
         compiler_params=vmem_params(12),
-        cost_estimate=pl.CostEstimate(flops=0, bytes_accessed=5 * MIB, transcendentals=0),
+        cost_estimate=pl.CostEstimate(flops=100_000_000, bytes_accessed=7 * MIB, transcendentals=0),
         name="weights",
-    )(rel_weight, token)
+    )(rel_weight, self_weight, features, token)
     partial_sum = pl.pallas_call(
         transform_kernel,
         out_shape=jax.ShapeDtypeStruct((width_all, width), jnp.float32),
         in_specs=[VMEM, VMEM, VMEM],
         out_specs=VMEM,
-        scratch_shapes=[pltpu.VMEM((relations * width_all, width), jnp.bfloat16)],
         compiler_params=vmem_params(8),
         name="transform",
     )(turned_weight, gathered, own)

time: 56.5 us -> 55.6 us (0.984)
  waiting for transfers between devices: 7.05 us -> 3.43 us
  starting transfers between devices: 33.8 us -> 36.4 us
  local copies, waits for them, and re-layouts: 3.66 us -> 2.75 us
  Pallas kernels: 11 us -> 11.9 us
    all_to_all x1, waiting for transfers between devices: 5.7 us -> 1.33 us  [shards(): lax.all_to_all(hidden, 'feat', split_axis=0, concat_axis=0, tiled=True, a...]
    ppermute x1, starting transfers between devices: 1.77 us -> 3.42 us  [shards(): other = lax.ppermute(partial_sum, 'rel', [(0, 1), (1, 0)])]
    pallas_call x2, Pallas kernels: 5.22 us -> 6.85 us  [the longest x1 4.54 us: shards(): pl.pallas_call(tiles_kernel, out_shape=jax.ShapeDtypeStruct((PADDED_PAIRS...]
    all_to_all x1, starting transfers between devices: 13.2 us -> 14.1 us  [shards(): lax.all_to_all(hidden, 'feat', split_axis=0, concat_axis=0, tiled=True, a...]
    unnamed x12, local copies, waits for them, and re-layouts: 3.66 us -> 2.75 us
    all_to_all x1, waiting for transfers between devices: 0.01 us -> 0.76 us  [shards(): lax.all_to_all(send, 'feat', split_axis=0, concat_axis=0, tiled=True, axi...]
  transfers between devices with their start and end apart: 3 -> 3, of which waited for: 2 -> 3; matrix products, arithmetic and copies ran while one was open for 0% -> 0% of each run, Pallas kernels for 9% -> 12%
where the time goes in v4:
time: 55.6 us; the launch traced here: 55.3 us
  starting transfers between devices  36.4 us (65%)
  Pallas kernels  11.9 us (21%)
  waiting for transfers between devices  3.43 us (6%)
  local copies, waits for them, and re-layouts  2.75 us (5%)
  other arithmetic  0.72 us (1%)
    all_to_all x1, starting transfers between devices, shards(): lax.all_to_all(send, 'feat', split_axis=0, concat_axis=0, tiled=True, axi...  18.8 us
    all_to_all x1, starting transfers between devices, shards(): lax.all_to_all(hidden, 'feat', split_axis=0, concat_axis=0, tiled=True, a...  14.1 us
    pallas_call x1, Pallas kernels, shards(): pl.pallas_call(tiles_kernel, out_shape=jax.ShapeDtypeStruct((PADDED_PAIRS...  4.54 us
    ppermute x1, starting transfers between devices, shards(): other = lax.ppermute(partial_sum, 'rel', [(0, 1), (1, 0)])  3.42 us
    unnamed x12, local copies, waits for them, and re-layouts  2.75 us
    pallas_call x1, Pallas kernels, shards(): pl.pallas_call(slots_kernel, out_shape=(jax.ShapeDtypeStruct((blocks, 4,...  2.41 us
    pallas_call x1, Pallas kernels, shards(): pl.pallas_call(weights_kernel, out_shape=(jax.ShapeDtypeStruct((width_all...  2.31 us
    pallas_call x1, Pallas kernels, shards(): pl.pallas_call(pack_kernel, out_shape=jax.ShapeDtypeStruct((blocks, heigh...  1.84 us
  transfers between devices with their start and end apart: 3, of which 3 were waited for; matrix products, arithmetic and copies ran while one was open for 0% of the time, Pallas kernels for 12%

profile of v4, /device:TPU:1, one launch (start us, length us, event | category | flops | bytes accessed | tf_op | source)
XLA Modules:
  0.0 55.3 jit_solution(3435566330665319325)
XLA Ops:
  0.0 1.8 %pack.1 = bf16[128,8,128]{2,1,0:T(8,128)(2,1)} custom-call(bf16[768,128]{1,0:T(8,128)(2,1)} %features_ref.3, s32[2,128]{1,0:T(2,128)} %degrees_ref.1), custom_call_target="tpu_custom_call" | custom-call | tf_op jit(solution)/shard_map/pack/pallas_call | solution.py:187
  1.8 18.8 %all-to-all-start = ((bf16[128,8,128]{2,1,0:T(8,128)(2,1)}), bf16[128,8,128]{2,1,0:T(8,128)(2,1)S(1)}, u32[]{:S(2)}, u32[]{:S(2)}) async-start(bf16[128,8,128]{2,1,0:T(8,128)(2,1)} %pack.1), calls=%async_computation | async-start | bytes 524288 | tf_op jit(solution)/shard_map/all_to_all | solution.py:196
  20.7 0.0 copy-start.3
  20.7 0.0 copy-start.4
  20.7 0.0 copy-start.5
  20.7 4.5 %tiles.1.tiles_ref = s8[80,128,256]{2,1,0:T(32,128)(4,1)S(1)} custom-call(s32[2,64,128,128]{3,2,1,0:T(8,128)} %tiles_ref.1), custom_call_target="tpu_custom_call" | custom-call | bytes 13631488 | tf_op jit(solution)/shard_map/tiles/pallas_call | solution.py:200
  25.3 0.0 copy-start.1
  25.3 0.8 %all-to-all-done.panels_ref = bf16[128,8,128]{2,1,0:T(8,128)(2,1)S(1)} async-done(((bf16[128,8,128]{2,1,0:T(8,128)(2,1)}), bf16[128,8,128]{2,1,0:T(8,128)(2,1)S(1)}, u32[]{:S(2)}, u32[]{:S(2)}) %all-to-all-start) | async-done | bytes 262176 | tf_op jit(solution)/shard_map/all_to_all | solution.py:196
  26.0 0.0 copy-done.3
  26.0 0.0 copy-done.4
  26.0 0.0 copy-done.5
  26.1 2.4 %slots.1 = (bf16[128,4,384]{2,1,0:T(4,128)(2,1)}, f32[8,128]{1,0:T(8,128)S(1)}) custom-call(s32[2,64]{1,0:T(2,128)S(1)} %copy-done.3, s32[2,64]{1,0:T(2,128)S(1)} %copy-done.4, s32[2]{0:T(128)S(1)} %copy-done.5, bf16[128,8,128]{2,1,0:T(8,128)(2,1)S(1)} %all-to-all-done.panels_ref, s8[80,128,256]{2,1,0:T(32,128)(4,1)S(1)} %tiles.1.tiles_ref), custom_call_target="tpu_custom_call" | custom-call | tf_op jit(solution)/shard_map/slots/pallas_call | solution.py:213
  28.5 14.1 %all-to-all-start.1 = ((bf16[128,4,384]{2,1,0:T(4,128)(2,1)}), bf16[128,4,384]{2,1,0:T(4,128)(2,1)S(1)}, u32[]{:S(2)}, u32[]{:S(2)}) async-start(bf16[128,4,384]{2,1,0:T(4,128)(2,1)} %get-tuple-element.11), calls=%async_computation.1 | async-start | bytes 786432 | tf_op jit(solution)/shard_map/all_to_all | solution.py:230
  42.6 0.0 copy-done.1
  42.6 0.0 copy-start
  42.6 1.7 %copy-done = bf16[2,768,768]{2,1,0:T(8,128)(2,1)S(1)} copy-done((bf16[2,768,768]{2,1,0:T(8,128)(2,1)S(1)}, bf16[2,768,768]{2,1,0:T(8,128)(2,1)}, u32[]{:S(2)}) %copy-start) | copy-done | bytes 2359320
  44.3 0.0 copy-start.2
  44.3 1.1 %copy-done.2 = bf16[384,768]{1,0:T(8,128)(2,1)S(1)} copy-done((bf16[384,768]{1,0:T(8,128)(2,1)S(1)}, bf16[384,768]{1,0:T(8,128)(2,1)}, u32[]{:S(2)}) %copy-start.2) | copy-done | bytes 589848
  45.3 2.3 %weights.1 = (bf16[768,1536]{1,0:T(8,128)(2,1)S(1)}, f32[768,128]{1,0:T(8,128)S(1)}) custom-call(bf16[2,768,768]{2,1,0:T(8,128)(2,1)S(1)} %copy-done, bf16[384,768]{1,0:T(8,128)(2,1)S(1)} %copy-done.2, bf16[768,128]{1,0:T(8,128)(2,1)S(1)} %copy-done.1, f32[8,128]{1,0:T(8,128)S(1)} %get-tuple-element.9.token_ref), custom_call_target="tpu_custom_call" | custom-call | flops 100000000 | bytes 7340032 | tf_op jit(solution)/shard_map/weights/pallas_call | solution.py:233
  47.7 1.3 %all-to-all-done.1.hidden_ref = bf16[128,4,384]{2,1,0:T(4,128)(2,1)S(1)} async-done(((bf16[128,4,384]{2,1,0:T(4,128)(2,1)}), bf16[128,4,384]{2,1,0:T(4,128)(2,1)S(1)}, u32[]{:S(2)}, u32[]{:S(2)}) %all-to-all-start.1) | async-done | bytes 393248 | tf_op jit(solution)/shard_map/all_to_all | solution.py:230
  49.0 0.8 %transform.1 = f32[768,128]{1,0:T(8,128)S(1)} custom-call(bf16[768,1536]{1,0:T(8,128)(2,1)S(1)} %get-tuple-element.10.turned_ref, bf16[128,4,384]{2,1,0:T(4,128)(2,1)S(1)} %all-to-all-done.1.hidden_ref, f32[768,128]{1,0:T(8,128)S(1)} %get-tuple-element.12.own_ref), custom_call_target="tpu_custom_call" | custom-call | tf_op jit(solution)/shard_map/transform/pallas_call | solution.py:245
  49.8 3.4 %collective-permute-start = (f32[768,128]{1,0:T(8,128)S(1)}, f32[768,128]{1,0:T(8,128)S(1)}, u32[]{:S(2)}, u32[]{:S(2)}) collective-permute-start(f32[768,128]{1,0:T(8,128)S(1)} %transform.1), channel_id=1, source_target_pairs={{0,1},{1,0},{2,3},{3,2},{4,5},{5,4},{6,7},{7,6},{8,9},{9,8},{10,11... | collective-permute-start | bytes 1179656 | tf_op jit(solution)/shard_map/ppermute | solution.py:253
  53.2 1.3 %collective-permute-done = f32[768,128]{1,0:T(8,128)S(1)} collective-permute-done((f32[768,128]{1,0:T(8,128)S(1)}, f32[768,128]{1,0:T(8,128)S(1)}, u32[]{:S(2)}, u32[]{:S(2)}) %collective-permute-start) | collective-permute-done | bytes 393248 | tf_op jit(solution)/shard_map/ppermute | solution.py:253
  54.6 0.7 %maximum_convert_fusion = bf16[768,128]{1,0:T(8,128)(2,1)} fusion(f32[768,128]{1,0:T(8,128)S(1)} %transform.1, f32[768,128]{1,0:T(8,128)S(1)} %collective-permute-done), kind=kLoop, calls=%fused_computation | loop fusion | flops 294912 | bytes 983040 | tf_op jit(solution)/shard_map/convert_element_type | solution.py:254
Async XLA Ops:
  1.8 24.2 %all-to-all-start = ((bf16[128,8,128]{2,1,0:T(8,128)(2,1)}), bf16[128,8,128]{2,1,0:T(8,128)(2,1)S(1)}, u32[]{:S(2)}, u32[]{:S(2)}) async-start(bf16[128,8,128]{2,1,0:T(8,128)(2,1)} %pack.1), calls=%async_computation | async-start | bytes 524288 | tf_op jit(solution)/shard_map/all_to_all | solution.py:196
  20.7 5.4 %copy-start.3 = (s32[2,64]{1,0:T(2,128)S(1)}, s32[2,64]{1,0:T(2,128)}, u32[]{:S(2)}) copy-start(s32[2,64]{1,0:T(2,128)} %rows_hbm.1) | copy-start | bytes 1540
  20.7 5.3 %copy-start.4 = (s32[2,64]{1,0:T(2,128)S(1)}, s32[2,64]{1,0:T(2,128)}, u32[]{:S(2)}) copy-start(s32[2,64]{1,0:T(2,128)} %cols_hbm.1) | copy-start | bytes 1540
  20.7 5.3 %copy-start.5 = (s32[2]{0:T(128)S(1)}, s32[2]{0:T(128)}, u32[]{:S(2)}) copy-start(s32[2]{0:T(128)} %live_hbm.1) | copy-start | bytes 28
  25.3 17.3 %copy-start.1 = (bf16[768,128]{1,0:T(8,128)(2,1)S(1)}, bf16[768,128]{1,0:T(8,128)(2,1)}, u32[]{:S(2)}) copy-start(bf16[768,128]{1,0:T(8,128)(2,1)} %features_ref.3) | copy-start | bytes 589828
  28.5 20.5 %all-to-all-start.1 = ((bf16[128,4,384]{2,1,0:T(4,128)(2,1)}), bf16[128,4,384]{2,1,0:T(4,128)(2,1)S(1)}, u32[]{:S(2)}, u32[]{:S(2)}) async-start(bf16[128,4,384]{2,1,0:T(4,128)(2,1)} %get-tuple-element.11), calls=%async_computation.1 | async-start | bytes 786432 | tf_op jit(solution)/shard_map/all_to_all | solution.py:230
  42.6 1.7 %copy-start = (bf16[2,768,768]{2,1,0:T(8,128)(2,1)S(1)}, bf16[2,768,768]{2,1,0:T(8,128)(2,1)}, u32[]{:S(2)}) copy-start(bf16[2,768,768]{2,1,0:T(8,128)(2,1)} %rel_ref.1) | copy-start | bytes 7077892
  44.3 1.1 %copy-start.2 = (bf16[384,768]{1,0:T(8,128)(2,1)S(1)}, bf16[384,768]{1,0:T(8,128)(2,1)}, u32[]{:S(2)}) copy-start(bf16[384,768]{1,0:T(8,128)(2,1)} %self_ref.1) | copy-start | bytes 1769476
  49.8 4.8 %collective-permute-start = (f32[768,128]{1,0:T(8,128)S(1)}, f32[768,128]{1,0:T(8,128)S(1)}, u32[]{:S(2)}, u32[]{:S(2)}) collective-permute-start(f32[768,128]{1,0:T(8,128)S(1)} %transform.1), channel_id=1, source_target_pairs={{0,1},{1,0},{2,3},{3,2},{4,5},{5,4},{6,7},{7,6},{8,9},{9,8},{10,11... | collective-permute-start | bytes 1179656 | tf_op jit(solution)/shard_map/ppermute | solution.py:253

commit v5 on v4

--- a/solution.py
+++ b/solution.py
@@ -9,8 +9,8 @@
 
 GROUP = 32
 CHUNK = 8
-PARTS = 1
-FIRST = 74
+PARTS = 2
+FIRST = 90
 PADDED_PAIRS = 80
 MIB = 1024 * 1024
 
@@ -32,7 +32,27 @@
         out_ref[start : start + 16] = (placed + tail[None]).astype(jnp.bfloat16)
 
 
-def tiles_kernel(tiles_ref, out_ref, landing_ref, arrived_ref):
+def hops(block, other):
+    total = 0
+    for size, stride in ((8, 16), (4, 4), (4, 1)):
+        apart = abs(block // stride % size - other // stride % size)
+        total += min(apart, size - apart)
+    return total
+
+
+def block_order(blocks):
+    rest = [block for block in range(blocks) if block != FIRST]
+    return [FIRST] + sorted(rest, key=lambda block: (-hops(block, FIRST), block))
+
+
+def positions(block, order):
+    found = jnp.zeros_like(block)
+    for index, member in enumerate(order):
+        found = jnp.where(block == member, index, found)
+    return found
+
+
+def tiles_kernel(tiles_ref, rows_ref, cols_ref, out_ref, row_at_ref, col_at_ref, landing_ref, arrived_ref):
     chunks, per_chunk = landing_ref.shape[0], landing_ref.shape[1]
     per_relation = tiles_ref.shape[1] // per_chunk
 
@@ -42,6 +62,9 @@
 
     for chunk in range(chunks):
         fetch(chunk).start()
+    order = block_order(128)
+    row_at_ref[...] = positions(rows_ref[...], order)
+    col_at_ref[...] = positions(cols_ref[...], order)
 
     def turn(chunk, carry):
         fetch(chunk).wait()
@@ -74,15 +97,12 @@
     take = height - relations
     pairs = rows_ref.shape[1] // 2
 
-    def position(block):
-        return jnp.bitwise_xor(block, FIRST)
-
     def add_group(relation, base, live):
         parts = []
         for step in range(0, GROUP, 2):
             slot = base + step
             panel = jnp.concatenate(
-                [panels_ref[position(cols_ref[relation, slot + side])] for side in range(2)], axis=0
+                [panels_ref[cols_ref[relation, slot + side]] for side in range(2)], axis=0
             )
             tile = tiles_ref[relation * pairs + slot // 2].astype(jnp.bfloat16)
             both = jnp.dot(panel, tile, preferred_element_type=jnp.float32)
@@ -90,7 +110,7 @@
         for step in range(GROUP):
             slot = base + step
             part = parts[step] if live is None else jnp.where(slot < live, parts[step], 0.0)
-            sums_ref[relation, position(rows_ref[relation, slot])] += part
+            sums_ref[relation, rows_ref[relation, slot]] += part
 
     for relation in range(relations):
         add_group(relation, 0, None)
@@ -120,7 +140,7 @@
             done_ref[at, :, 2 * width : 3 * width] = rest.astype(jnp.bfloat16)
             return carry
 
-        lax.fori_loop(0, part_blocks // 8, finish, 0)
+        lax.fori_loop(0, part_blocks // 8, finish, 0, unroll=4)
         store(part).start()
     for part in range(PARTS):
         store(part).wait()
@@ -192,16 +212,20 @@
         compiler_params=vmem_params(62),
         name="pack",
     )(features, degrees)
-    order = [[FIRST ^ index for index in range(blocks)]]
+    order = [block_order(blocks)]
     panels = lax.all_to_all(
         send, "feat", split_axis=0, concat_axis=0, tiled=True, axis_index_groups=order
     )
     chunks = relations * slots // CHUNK
-    tiles = pl.pallas_call(
+    tiles, row_at, col_at = pl.pallas_call(
         tiles_kernel,
-        out_shape=jax.ShapeDtypeStruct((PADDED_PAIRS, block_size, 2 * block_size), jnp.int8),
-        in_specs=[ANY],
-        out_specs=VMEM,
+        out_shape=(
+            jax.ShapeDtypeStruct((PADDED_PAIRS, block_size, 2 * block_size), jnp.int8),
+            jax.ShapeDtypeStruct(block_rows.shape, jnp.int32),
+            jax.ShapeDtypeStruct(block_cols.shape, jnp.int32),
+        ),
+        in_specs=[ANY, VMEM, VMEM],
+        out_specs=(VMEM, VMEM, VMEM),
         scratch_shapes=[
             pltpu.VMEM((chunks, CHUNK, block_size, block_size), jnp.int32),
             DMA((chunks,)),
@@ -209,7 +233,7 @@
         compiler_params=vmem_params(50),
         cost_estimate=pl.CostEstimate(flops=0, bytes_accessed=13 * MIB, transcendentals=0),
         name="tiles",
-    )(count_tiles)
+    )(count_tiles, block_rows, block_cols)
     hidden, token = pl.pallas_call(
         slots_kernel,
         out_shape=(jax.ShapeDtypeStruct((blocks, 4, 3 * width), jnp.bfloat16), TOKEN),
@@ -226,7 +250,7 @@
         ],
         compiler_params=vmem_params(8),
         name="slots",
-    )(block_rows, block_cols, live_slots, panels, tiles)
+    )(row_at, col_at, live_slots, panels, tiles)
     gathered = lax.all_to_all(
         hidden, "feat", split_axis=0, concat_axis=0, tiled=True, axis_index_groups=order
     )

time: 55.6 us -> 54.9 us (0.987)
  starting transfers between devices: 36.4 us -> 32.6 us
  waiting for transfers between devices: 3.43 us -> 5.24 us
  local copies, waits for them, and re-layouts: 2.75 us -> 4.09 us
    all_to_all x1, waiting for transfers between devices: 1.33 us -> 3.41 us  [shards(): lax.all_to_all(hidden, 'feat', split_axis=0, concat_axis=0, tiled=True, a...]
    ppermute x1, starting transfers between devices: 3.42 us -> 1.87 us  [shards(): other = lax.ppermute(partial_sum, 'rel', [(0, 1), (1, 0)])]
    unnamed x12, local copies, waits for them, and re-layouts: 2.75 us -> 4.09 us
    all_to_all x1, starting transfers between devices: 18.8 us -> 17.5 us  [shards(): lax.all_to_all(send, 'feat', split_axis=0, concat_axis=0, tiled=True, axi...]
    all_to_all x1, starting transfers between devices: 14.1 us -> 13.2 us  [shards(): lax.all_to_all(hidden, 'feat', split_axis=0, concat_axis=0, tiled=True, a...]
  transfers between devices with their start and end apart: 3 -> 3, of which waited for: 3 -> 3; matrix products, arithmetic and copies ran while one was open for 0% -> 0% of each run, Pallas kernels for 12% -> 13%
where the time goes in v5:
time: 54.9 us; the launch traced here: 54.4 us
  starting transfers between devices  32.6 us (59%)
  Pallas kernels  11.7 us (21%)
  waiting for transfers between devices  5.24 us (10%)
  local copies, waits for them, and re-layouts  4.09 us (7%)
  other arithmetic  0.72 us (1%)
    all_to_all x1, starting transfers between devices, shards(): lax.all_to_all(send, 'feat', split_axis=0, concat_axis=0, tiled=True, axi...  17.5 us
    all_to_all x1, starting transfers between devices, shards(): lax.all_to_all(hidden, 'feat', split_axis=0, concat_axis=0, tiled=True, a...  13.2 us
    pallas_call x1, Pallas kernels, shards(): pl.pallas_call(tiles_kernel, out_shape=(jax.ShapeDtypeStruct((PADDED_PAIR...  4.54 us
    unnamed x12, local copies, waits for them, and re-layouts  4.09 us
    all_to_all x1, waiting for transfers between devices, shards(): lax.all_to_all(hidden, 'feat', split_axis=0, concat_axis=0, tiled=True, a...  3.41 us
    pallas_call x1, Pallas kernels, shards(): pl.pallas_call(weights_kernel, out_shape=(jax.ShapeDtypeStruct((width_all...  2.31 us
    pallas_call x1, Pallas kernels, shards(): pl.pallas_call(slots_kernel, out_shape=(jax.ShapeDtypeStruct((blocks, 4,...  2.24 us
    ppermute x1, starting transfers between devices, shards(): other = lax.ppermute(partial_sum, 'rel', [(0, 1), (1, 0)])  1.87 us
  transfers between devices with their start and end apart: 3, of which 3 were waited for; matrix products, arithmetic and copies ran while one was open for 0% of the time, Pallas kernels for 13%

profile of v5, /device:TPU:1, one launch (start us, length us, event | category | flops | bytes accessed | tf_op | source)
XLA Modules:
  0.0 54.4 jit_solution(17902825385385696450)
XLA Ops:
  0.0 1.8 %pack.1 = bf16[128,8,128]{2,1,0:T(8,128)(2,1)} custom-call(bf16[768,128]{1,0:T(8,128)(2,1)} %features_ref.3, s32[2,128]{1,0:T(2,128)} %degrees_ref.1), custom_call_target="tpu_custom_call" | custom-call | tf_op jit(solution)/shard_map/pack/pallas_call | solution.py:207
  1.8 17.5 %all-to-all-start = ((bf16[128,8,128]{2,1,0:T(8,128)(2,1)}), bf16[128,8,128]{2,1,0:T(8,128)(2,1)S(1)}, u32[]{:S(2)}, u32[]{:S(2)}) async-start(bf16[128,8,128]{2,1,0:T(8,128)(2,1)} %pack.1), calls=%async_computation | async-start | bytes 524288 | tf_op jit(solution)/shard_map/all_to_all | solution.py:216
  19.4 0.0 copy-start.3
  19.4 0.7 %copy-done.3 = s32[2,64]{1,0:T(2,128)S(1)} copy-done((s32[2,64]{1,0:T(2,128)S(1)}, s32[2,64]{1,0:T(2,128)}, u32[]{:S(2)}) %copy-start.3) | copy-done | bytes 536
  20.1 0.0 copy-start.4
  20.1 0.7 %copy-done.4 = s32[2,64]{1,0:T(2,128)S(1)} copy-done((s32[2,64]{1,0:T(2,128)S(1)}, s32[2,64]{1,0:T(2,128)}, u32[]{:S(2)}) %copy-start.4) | copy-done | bytes 536
  20.8 0.0 copy-start.5
  20.8 4.5 %tiles.1 = (s8[80,128,256]{2,1,0:T(32,128)(4,1)S(1)}, s32[2,64]{1,0:T(2,128)S(1)}, s32[2,64]{1,0:T(2,128)S(1)}) custom-call(s32[2,64,128,128]{3,2,1,0:T(8,128)} %tiles_ref.1, s32[2,64]{1,0:T(2,128)S(1)} %copy-done.3, s32[2,64]{1,0:T(2,128)S(1)} %copy-done.4), custom_call_target="tpu_custom_call" | custom-call | bytes 13631488 | tf_op jit(solution)/shard_map/tiles/pallas_call | solution.py:220
  25.3 0.0 copy-start.1
  25.3 0.5 all-to-all-done.panels_ref
  25.8 0.0 copy-done.5
  25.8 2.2 %slots.1 = (bf16[128,4,384]{2,1,0:T(4,128)(2,1)}, f32[8,128]{1,0:T(8,128)S(1)}) custom-call(s32[2,64]{1,0:T(2,128)S(1)} %get-tuple-element.12.rows_hbm, s32[2,64]{1,0:T(2,128)S(1)} %get-tuple-element.13.cols_hbm, s32[2]{0:T(128)S(1)} %copy-done.5, bf16[128,8,128]{2,1,0:T(8,128)(2,1)S(1)} %all-to-all-done.panels_ref, ...), custom_call_target="tpu_custom_call" | custom-call | tf_op jit(solution)/shard_map/slots/pallas_call | solution.py:237
  28.1 13.2 %all-to-all-start.1 = ((bf16[128,4,384]{2,1,0:T(4,128)(2,1)}), bf16[128,4,384]{2,1,0:T(4,128)(2,1)S(1)}, u32[]{:S(2)}, u32[]{:S(2)}) async-start(bf16[128,4,384]{2,1,0:T(4,128)(2,1)} %get-tuple-element.17), calls=%async_computation.1 | async-start | bytes 786432 | tf_op jit(solution)/shard_map/all_to_all | solution.py:254
  41.2 0.0 copy-done.1
  41.2 0.0 copy-start
  41.2 1.7 %copy-done = bf16[2,768,768]{2,1,0:T(8,128)(2,1)S(1)} copy-done((bf16[2,768,768]{2,1,0:T(8,128)(2,1)S(1)}, bf16[2,768,768]{2,1,0:T(8,128)(2,1)}, u32[]{:S(2)}) %copy-start) | copy-done | bytes 2359320
  42.9 0.0 copy-start.2
  42.9 1.1 %copy-done.2 = bf16[384,768]{1,0:T(8,128)(2,1)S(1)} copy-done((bf16[384,768]{1,0:T(8,128)(2,1)S(1)}, bf16[384,768]{1,0:T(8,128)(2,1)}, u32[]{:S(2)}) %copy-start.2) | copy-done | bytes 589848
  44.0 2.3 %weights.1 = (bf16[768,1536]{1,0:T(8,128)(2,1)S(1)}, f32[768,128]{1,0:T(8,128)S(1)}) custom-call(bf16[2,768,768]{2,1,0:T(8,128)(2,1)S(1)} %copy-done, bf16[384,768]{1,0:T(8,128)(2,1)S(1)} %copy-done.2, bf16[768,128]{1,0:T(8,128)(2,1)S(1)} %copy-done.1, f32[8,128]{1,0:T(8,128)S(1)} %get-tuple-element.15.token_ref), custom_call_target="tpu_custom_call" | custom-call | flops 100000000 | bytes 7340032 | tf_op jit(solution)/shard_map/weights/pallas_call | solution.py:257
  46.3 3.4 %all-to-all-done.1.hidden_ref = bf16[128,4,384]{2,1,0:T(4,128)(2,1)S(1)} async-done(((bf16[128,4,384]{2,1,0:T(4,128)(2,1)}), bf16[128,4,384]{2,1,0:T(4,128)(2,1)S(1)}, u32[]{:S(2)}, u32[]{:S(2)}) %all-to-all-start.1) | async-done | bytes 393248 | tf_op jit(solution)/shard_map/all_to_all | solution.py:254
  49.7 0.8 %transform.1 = f32[768,128]{1,0:T(8,128)S(1)} custom-call(bf16[768,1536]{1,0:T(8,128)(2,1)S(1)} %get-tuple-element.16.turned_ref, bf16[128,4,384]{2,1,0:T(4,128)(2,1)S(1)} %all-to-all-done.1.hidden_ref, f32[768,128]{1,0:T(8,128)S(1)} %get-tuple-element.18.own_ref), custom_call_target="tpu_custom_call" | custom-call | tf_op jit(solution)/shard_map/transform/pallas_call | solution.py:269
  50.5 1.9 %collective-permute-start = (f32[768,128]{1,0:T(8,128)S(1)}, f32[768,128]{1,0:T(8,128)S(1)}, u32[]{:S(2)}, u32[]{:S(2)}) collective-permute-start(f32[768,128]{1,0:T(8,128)S(1)} %transform.1), channel_id=1, source_target_pairs={{0,1},{1,0},{2,3},{3,2},{4,5},{5,4},{6,7},{7,6},{8,9},{9,8},{10,11... | collective-permute-start | bytes 1179656 | tf_op jit(solution)/shard_map/ppermute | solution.py:277
  52.4 1.3 %collective-permute-done = f32[768,128]{1,0:T(8,128)S(1)} collective-permute-done((f32[768,128]{1,0:T(8,128)S(1)}, f32[768,128]{1,0:T(8,128)S(1)}, u32[]{:S(2)}, u32[]{:S(2)}) %collective-permute-start) | collective-permute-done | bytes 393248 | tf_op jit(solution)/shard_map/ppermute | solution.py:277
  53.7 0.7 %maximum_convert_fusion = bf16[768,128]{1,0:T(8,128)(2,1)} fusion(f32[768,128]{1,0:T(8,128)S(1)} %transform.1, f32[768,128]{1,0:T(8,128)S(1)} %collective-permute-done), kind=kLoop, calls=%fused_computation | loop fusion | flops 294912 | bytes 983040 | tf_op jit(solution)/shard_map/convert_element_type | solution.py:278
Async XLA Ops:
  1.8 24.0 %all-to-all-start = ((bf16[128,8,128]{2,1,0:T(8,128)(2,1)}), bf16[128,8,128]{2,1,0:T(8,128)(2,1)S(1)}, u32[]{:S(2)}, u32[]{:S(2)}) async-start(bf16[128,8,128]{2,1,0:T(8,128)(2,1)} %pack.1), calls=%async_computation | async-start | bytes 524288 | tf_op jit(solution)/shard_map/all_to_all | solution.py:216
  19.4 0.7 %copy-start.3 = (s32[2,64]{1,0:T(2,128)S(1)}, s32[2,64]{1,0:T(2,128)}, u32[]{:S(2)}) copy-start(s32[2,64]{1,0:T(2,128)} %rows_ref.1) | copy-start | bytes 1540
  20.1 0.7 %copy-start.4 = (s32[2,64]{1,0:T(2,128)S(1)}, s32[2,64]{1,0:T(2,128)}, u32[]{:S(2)}) copy-start(s32[2,64]{1,0:T(2,128)} %cols_ref.1) | copy-start | bytes 1540
  20.8 5.0 %copy-start.5 = (s32[2]{0:T(128)S(1)}, s32[2]{0:T(128)}, u32[]{:S(2)}) copy-start(s32[2]{0:T(128)} %live_hbm.1) | copy-start | bytes 28
  25.3 15.9 %copy-start.1 = (bf16[768,128]{1,0:T(8,128)(2,1)S(1)}, bf16[768,128]{1,0:T(8,128)(2,1)}, u32[]{:S(2)}) copy-start(bf16[768,128]{1,0:T(8,128)(2,1)} %features_ref.3) | copy-start | bytes 589828
  28.1 21.6 %all-to-all-start.1 = ((bf16[128,4,384]{2,1,0:T(4,128)(2,1)}), bf16[128,4,384]{2,1,0:T(4,128)(2,1)S(1)}, u32[]{:S(2)}, u32[]{:S(2)}) async-start(bf16[128,4,384]{2,1,0:T(4,128)(2,1)} %get-tuple-element.17), calls=%async_computation.1 | async-start | bytes 786432 | tf_op jit(solution)/shard_map/all_to_all | solution.py:254
  41.2 1.7 %copy-start = (bf16[2,768,768]{2,1,0:T(8,128)(2,1)S(1)}, bf16[2,768,768]{2,1,0:T(8,128)(2,1)}, u32[]{:S(2)}) copy-start(bf16[2,768,768]{2,1,0:T(8,128)(2,1)} %rel_ref.1) | copy-start | bytes 7077892
  42.9 1.1 %copy-start.2 = (bf16[384,768]{1,0:T(8,128)(2,1)S(1)}, bf16[384,768]{1,0:T(8,128)(2,1)}, u32[]{:S(2)}) copy-start(bf16[384,768]{1,0:T(8,128)(2,1)} %self_ref.1) | copy-start | bytes 1769476
  50.5 3.2 %collective-permute-start = (f32[768,128]{1,0:T(8,128)S(1)}, f32[768,128]{1,0:T(8,128)S(1)}, u32[]{:S(2)}, u32[]{:S(2)}) collective-permute-start(f32[768,128]{1,0:T(8,128)S(1)} %transform.1), channel_id=1, source_target_pairs={{0,1},{1,0},{2,3},{3,2},{4,5},{5,4},{6,7},{7,6},{8,9},{9,8},{10,11... | collective-permute-start | bytes 1179656 | tf_op jit(solution)/shard_map/ppermute | solution.py:277

commit v6 on v5

--- a/solution.py
+++ b/solution.py
@@ -79,7 +79,7 @@
 
 def slots_kernel(
     rows_hbm, cols_hbm, live_hbm, panels_ref, tiles_ref, out_ref, token_ref,
-    rows_ref, cols_ref, live_ref, sums_ref, done_ref, in_sem, out_sem,
+    rows_ref, cols_ref, live_ref, inverse_ref, sums_ref, done_ref, in_sem, out_sem,
 ):
     pulls = [
         pltpu.make_async_copy(source, target, in_sem.at[index])
@@ -91,10 +91,11 @@
         pull.start()
     token_ref[...] = jnp.zeros_like(token_ref)
     sums_ref[...] = jnp.zeros_like(sums_ref)
+    relations, blocks, height, width = sums_ref.shape
+    take = height - relations
+    inverse_ref[...] = 1.0 / panels_ref[:, take:height, :].astype(jnp.float32)
     for pull in pulls:
         pull.wait()
-    relations, blocks, height, width = sums_ref.shape
-    take = height - relations
     pairs = rows_ref.shape[1] // 2
 
     def add_group(relation, base, live):
@@ -129,9 +130,9 @@
 
         def finish(index, carry, part=part):
             at = pl.ds(part * part_blocks + index * 8, 8)
-            packed = panels_ref[at].astype(jnp.float32)
+            inverse = inverse_ref[at]
             first, second = [
-                sums_ref[relation, at] / packed[:, take + relation : take + relation + 1, :]
+                sums_ref[relation, at] * inverse[:, relation : relation + 1, :]
                 for relation in range(2)
             ]
             rest = jnp.concatenate([first[:, 4:6], second[:, 4:6]], axis=1)
@@ -243,6 +244,7 @@
             pltpu.SMEM(block_rows.shape, jnp.int32),
             pltpu.SMEM(block_cols.shape, jnp.int32),
             pltpu.SMEM(live_slots.shape, jnp.int32),
+            pltpu.VMEM((blocks, relations, width), jnp.float32),
             pltpu.VMEM((relations, blocks, height, width), jnp.float32),
             pltpu.VMEM((blocks, 4, 3 * width), jnp.bfloat16),
             DMA((3,)),

time: 54.9 us -> 54.7 us (level)
  no operation moved by 1% of the time
where the time goes in v6:
time: 54.7 us; the launch traced here: 54.4 us
  starting transfers between devices  32.6 us (60%)
  Pallas kernels  11.7 us (21%)
  waiting for transfers between devices  5.25 us (10%)
  local copies, waits for them, and re-layouts  4.09 us (7%)
  other arithmetic  0.72 us (1%)
    all_to_all x1, starting transfers between devices, shards(): lax.all_to_all(send, 'feat', split_axis=0, concat_axis=0, tiled=True, axi...  17.5 us
    all_to_all x1, starting transfers between devices, shards(): lax.all_to_all(hidden, 'feat', split_axis=0, concat_axis=0, tiled=True, a...  13.2 us
    pallas_call x1, Pallas kernels, shards(): pl.pallas_call(tiles_kernel, out_shape=(jax.ShapeDtypeStruct((PADDED_PAIR...  4.54 us
    unnamed x12, local copies, waits for them, and re-layouts  4.09 us
    all_to_all x1, waiting for transfers between devices, shards(): lax.all_to_all(hidden, 'feat', split_axis=0, concat_axis=0, tiled=True, a...  3.41 us
    pallas_call x1, Pallas kernels, shards(): pl.pallas_call(weights_kernel, out_shape=(jax.ShapeDtypeStruct((width_all...  2.31 us
    pallas_call x1, Pallas kernels, shards(): pl.pallas_call(slots_kernel, out_shape=(jax.ShapeDtypeStruct((blocks, 4,...  2.17 us
    ppermute x1, starting transfers between devices, shards(): other = lax.ppermute(partial_sum, 'rel', [(0, 1), (1, 0)])  1.86 us
  transfers between devices with their start and end apart: 3, of which 3 were waited for; matrix products, arithmetic and copies ran while one was open for 0% of the time, Pallas kernels for 13%

profile of v6, /device:TPU:1, one launch (start us, length us, event | category | flops | bytes accessed | tf_op | source)
XLA Modules:
  0.0 54.4 jit_solution(12962005608962333912)
XLA Ops:
  0.0 1.8 %pack.1 = bf16[128,8,128]{2,1,0:T(8,128)(2,1)} custom-call(bf16[768,128]{1,0:T(8,128)(2,1)} %features_ref.3, s32[2,128]{1,0:T(2,128)} %degrees_ref.1), custom_call_target="tpu_custom_call" | custom-call | tf_op jit(solution)/shard_map/pack/pallas_call | solution.py:208
  1.8 17.5 %all-to-all-start = ((bf16[128,8,128]{2,1,0:T(8,128)(2,1)}), bf16[128,8,128]{2,1,0:T(8,128)(2,1)S(1)}, u32[]{:S(2)}, u32[]{:S(2)}) async-start(bf16[128,8,128]{2,1,0:T(8,128)(2,1)} %pack.1), calls=%async_computation | async-start | bytes 524288 | tf_op jit(solution)/shard_map/all_to_all | solution.py:217
  19.4 0.0 copy-start.3
  19.4 0.7 %copy-done.3 = s32[2,64]{1,0:T(2,128)S(1)} copy-done((s32[2,64]{1,0:T(2,128)S(1)}, s32[2,64]{1,0:T(2,128)}, u32[]{:S(2)}) %copy-start.3) | copy-done | bytes 536
  20.1 0.0 copy-start.4
  20.1 0.7 %copy-done.4 = s32[2,64]{1,0:T(2,128)S(1)} copy-done((s32[2,64]{1,0:T(2,128)S(1)}, s32[2,64]{1,0:T(2,128)}, u32[]{:S(2)}) %copy-start.4) | copy-done | bytes 536
  20.8 0.0 copy-start.5
  20.8 4.5 %tiles.1 = (s8[80,128,256]{2,1,0:T(32,128)(4,1)S(1)}, s32[2,64]{1,0:T(2,128)S(1)}, s32[2,64]{1,0:T(2,128)S(1)}) custom-call(s32[2,64,128,128]{3,2,1,0:T(8,128)} %tiles_ref.1, s32[2,64]{1,0:T(2,128)S(1)} %copy-done.3, s32[2,64]{1,0:T(2,128)S(1)} %copy-done.4), custom_call_target="tpu_custom_call" | custom-call | bytes 13631488 | tf_op jit(solution)/shard_map/tiles/pallas_call | solution.py:221
  25.3 0.0 copy-start.1
  25.3 0.5 all-to-all-done.panels_ref
  25.8 0.0 copy-done.5
  25.8 2.2 %slots.1 = (bf16[128,4,384]{2,1,0:T(4,128)(2,1)}, f32[8,128]{1,0:T(8,128)S(1)}) custom-call(s32[2,64]{1,0:T(2,128)S(1)} %get-tuple-element.12.rows_hbm, s32[2,64]{1,0:T(2,128)S(1)} %get-tuple-element.13.cols_hbm, s32[2]{0:T(128)S(1)} %copy-done.5, bf16[128,8,128]{2,1,0:T(8,128)(2,1)S(1)} %all-to-all-done.panels_ref, ...), custom_call_target="tpu_custom_call" | custom-call | tf_op jit(solution)/shard_map/slots/pallas_call | solution.py:238
  28.0 13.2 %all-to-all-start.1 = ((bf16[128,4,384]{2,1,0:T(4,128)(2,1)}), bf16[128,4,384]{2,1,0:T(4,128)(2,1)S(1)}, u32[]{:S(2)}, u32[]{:S(2)}) async-start(bf16[128,4,384]{2,1,0:T(4,128)(2,1)} %get-tuple-element.17), calls=%async_computation.1 | async-start | bytes 786432 | tf_op jit(solution)/shard_map/all_to_all | solution.py:256
  41.1 0.0 copy-done.1
  41.2 0.0 copy-start
  41.2 1.7 %copy-done = bf16[2,768,768]{2,1,0:T(8,128)(2,1)S(1)} copy-done((bf16[2,768,768]{2,1,0:T(8,128)(2,1)S(1)}, bf16[2,768,768]{2,1,0:T(8,128)(2,1)}, u32[]{:S(2)}) %copy-start) | copy-done | bytes 2359320
  42.8 0.0 copy-start.2
  42.8 1.1 %copy-done.2 = bf16[384,768]{1,0:T(8,128)(2,1)S(1)} copy-done((bf16[384,768]{1,0:T(8,128)(2,1)S(1)}, bf16[384,768]{1,0:T(8,128)(2,1)}, u32[]{:S(2)}) %copy-start.2) | copy-done | bytes 589848
  43.9 2.3 %weights.1 = (bf16[768,1536]{1,0:T(8,128)(2,1)S(1)}, f32[768,128]{1,0:T(8,128)S(1)}) custom-call(bf16[2,768,768]{2,1,0:T(8,128)(2,1)S(1)} %copy-done, bf16[384,768]{1,0:T(8,128)(2,1)S(1)} %copy-done.2, bf16[768,128]{1,0:T(8,128)(2,1)S(1)} %copy-done.1, f32[8,128]{1,0:T(8,128)S(1)} %get-tuple-element.15.token_ref), custom_call_target="tpu_custom_call" | custom-call | flops 100000000 | bytes 7340032 | tf_op jit(solution)/shard_map/weights/pallas_call | solution.py:259
  46.2 3.4 %all-to-all-done.1.hidden_ref = bf16[128,4,384]{2,1,0:T(4,128)(2,1)S(1)} async-done(((bf16[128,4,384]{2,1,0:T(4,128)(2,1)}), bf16[128,4,384]{2,1,0:T(4,128)(2,1)S(1)}, u32[]{:S(2)}, u32[]{:S(2)}) %all-to-all-start.1) | async-done | bytes 393248 | tf_op jit(solution)/shard_map/all_to_all | solution.py:256
  49.6 0.8 %transform.1 = f32[768,128]{1,0:T(8,128)S(1)} custom-call(bf16[768,1536]{1,0:T(8,128)(2,1)S(1)} %get-tuple-element.16.turned_ref, bf16[128,4,384]{2,1,0:T(4,128)(2,1)S(1)} %all-to-all-done.1.hidden_ref, f32[768,128]{1,0:T(8,128)S(1)} %get-tuple-element.18.own_ref), custom_call_target="tpu_custom_call" | custom-call | tf_op jit(solution)/shard_map/transform/pallas_call | solution.py:271
  50.4 1.9 %collective-permute-start = (f32[768,128]{1,0:T(8,128)S(1)}, f32[768,128]{1,0:T(8,128)S(1)}, u32[]{:S(2)}, u32[]{:S(2)}) collective-permute-start(f32[768,128]{1,0:T(8,128)S(1)} %transform.1), channel_id=1, source_target_pairs={{0,1},{1,0},{2,3},{3,2},{4,5},{5,4},{6,7},{7,6},{8,9},{9,8},{10,11... | collective-permute-start | bytes 1179656 | tf_op jit(solution)/shard_map/ppermute | solution.py:279
  52.3 1.3 %collective-permute-done = f32[768,128]{1,0:T(8,128)S(1)} collective-permute-done((f32[768,128]{1,0:T(8,128)S(1)}, f32[768,128]{1,0:T(8,128)S(1)}, u32[]{:S(2)}, u32[]{:S(2)}) %collective-permute-start) | collective-permute-done | bytes 393248 | tf_op jit(solution)/shard_map/ppermute | solution.py:279
  53.6 0.7 %maximum_convert_fusion = bf16[768,128]{1,0:T(8,128)(2,1)} fusion(f32[768,128]{1,0:T(8,128)S(1)} %transform.1, f32[768,128]{1,0:T(8,128)S(1)} %collective-permute-done), kind=kLoop, calls=%fused_computation | loop fusion | flops 294912 | bytes 983040 | tf_op jit(solution)/shard_map/convert_element_type | solution.py:280
Async XLA Ops:
  1.8 24.0 %all-to-all-start = ((bf16[128,8,128]{2,1,0:T(8,128)(2,1)}), bf16[128,8,128]{2,1,0:T(8,128)(2,1)S(1)}, u32[]{:S(2)}, u32[]{:S(2)}) async-start(bf16[128,8,128]{2,1,0:T(8,128)(2,1)} %pack.1), calls=%async_computation | async-start | bytes 524288 | tf_op jit(solution)/shard_map/all_to_all | solution.py:217
  19.4 0.7 %copy-start.3 = (s32[2,64]{1,0:T(2,128)S(1)}, s32[2,64]{1,0:T(2,128)}, u32[]{:S(2)}) copy-start(s32[2,64]{1,0:T(2,128)} %rows_ref.1) | copy-start | bytes 1540
  20.1 0.7 %copy-start.4 = (s32[2,64]{1,0:T(2,128)S(1)}, s32[2,64]{1,0:T(2,128)}, u32[]{:S(2)}) copy-start(s32[2,64]{1,0:T(2,128)} %cols_ref.1) | copy-start | bytes 1540
  20.8 5.0 %copy-start.5 = (s32[2]{0:T(128)S(1)}, s32[2]{0:T(128)}, u32[]{:S(2)}) copy-start(s32[2]{0:T(128)} %live_hbm.1) | copy-start | bytes 28
  25.3 15.8 %copy-start.1 = (bf16[768,128]{1,0:T(8,128)(2,1)S(1)}, bf16[768,128]{1,0:T(8,128)(2,1)}, u32[]{:S(2)}) copy-start(bf16[768,128]{1,0:T(8,128)(2,1)} %features_ref.3) | copy-start | bytes 589828
  28.0 21.6 %all-to-all-start.1 = ((bf16[128,4,384]{2,1,0:T(4,128)(2,1)}), bf16[128,4,384]{2,1,0:T(4,128)(2,1)S(1)}, u32[]{:S(2)}, u32[]{:S(2)}) async-start(bf16[128,4,384]{2,1,0:T(4,128)(2,1)} %get-tuple-element.17), calls=%async_computation.1 | async-start | bytes 786432 | tf_op jit(solution)/shard_map/all_to_all | solution.py:256
  41.2 1.7 %copy-start = (bf16[2,768,768]{2,1,0:T(8,128)(2,1)S(1)}, bf16[2,768,768]{2,1,0:T(8,128)(2,1)}, u32[]{:S(2)}) copy-start(bf16[2,768,768]{2,1,0:T(8,128)(2,1)} %rel_ref.1) | copy-start | bytes 7077892
  42.8 1.1 %copy-start.2 = (bf16[384,768]{1,0:T(8,128)(2,1)S(1)}, bf16[384,768]{1,0:T(8,128)(2,1)}, u32[]{:S(2)}) copy-start(bf16[384,768]{1,0:T(8,128)(2,1)} %self_ref.1) | copy-start | bytes 1769476
  50.4 3.2 %collective-permute-start = (f32[768,128]{1,0:T(8,128)S(1)}, f32[768,128]{1,0:T(8,128)S(1)}, u32[]{:S(2)}, u32[]{:S(2)}) collective-permute-start(f32[768,128]{1,0:T(8,128)S(1)} %transform.1), channel_id=1, source_target_pairs={{0,1},{1,0},{2,3},{3,2},{4,5},{5,4},{6,7},{7,6},{8,9},{9,8},{10,11... | collective-permute-start | bytes 1179656 | tf_op jit(solution)/shard_map/ppermute | solution.py:279

commit v7 on v6

--- a/solution.py
+++ b/solution.py
@@ -141,7 +141,7 @@
             done_ref[at, :, 2 * width : 3 * width] = rest.astype(jnp.bfloat16)
             return carry
 
-        lax.fori_loop(0, part_blocks // 8, finish, 0, unroll=4)
+        lax.fori_loop(0, part_blocks // 8, finish, 0, unroll=8)
         store(part).start()
     for part in range(PARTS):
         store(part).wait()

time: 54.7 us -> 55 us (level)
  no operation moved by 1% of the time
where the time goes in v7:
time: 55 us; the launch traced here: 54.6 us
  starting transfers between devices  32.3 us (59%)
  Pallas kernels  11.9 us (22%)
  waiting for transfers between devices  5.51 us (10%)
  local copies, waits for them, and re-layouts  4.09 us (7%)
  other arithmetic  0.72 us (1%)
    all_to_all x1, starting transfers between devices, shards(): lax.all_to_all(send, 'feat', split_axis=0, concat_axis=0, tiled=True, axi...  17.5 us
    all_to_all x1, starting transfers between devices, shards(): lax.all_to_all(hidden, 'feat', split_axis=0, concat_axis=0, tiled=True, a...  13.2 us
    pallas_call x1, Pallas kernels, shards(): pl.pallas_call(tiles_kernel, out_shape=(jax.ShapeDtypeStruct((PADDED_PAIR...  4.54 us
    unnamed x12, local copies, waits for them, and re-layouts  4.09 us
    all_to_all x1, waiting for transfers between devices, shards(): lax.all_to_all(hidden, 'feat', split_axis=0, concat_axis=0, tiled=True, a...  3.68 us
    pallas_call x1, Pallas kernels, shards(): pl.pallas_call(slots_kernel, out_shape=(jax.ShapeDtypeStruct((blocks, 4,...  2.43 us
    pallas_call x1, Pallas kernels, shards(): pl.pallas_call(weights_kernel, out_shape=(jax.ShapeDtypeStruct((width_all...  2.31 us
    pallas_call x1, Pallas kernels, shards(): pl.pallas_call(pack_kernel, out_shape=jax.ShapeDtypeStruct((blocks, heigh...  1.83 us
  transfers between devices with their start and end apart: 3, of which 3 were waited for; matrix products, arithmetic and copies ran while one was open for 0% of the time, Pallas kernels for 13%

profile of v7, /device:TPU:1, one launch (start us, length us, event | category | flops | bytes accessed | tf_op | source)
XLA Modules:
  0.0 54.6 jit_solution(9132138462382439396)
XLA Ops:
  0.0 1.8 %pack.1 = bf16[128,8,128]{2,1,0:T(8,128)(2,1)} custom-call(bf16[768,128]{1,0:T(8,128)(2,1)} %features_ref.3, s32[2,128]{1,0:T(2,128)} %degrees_ref.1), custom_call_target="tpu_custom_call" | custom-call | tf_op jit(solution)/shard_map/pack/pallas_call | solution.py:208
  1.8 17.5 %all-to-all-start = ((bf16[128,8,128]{2,1,0:T(8,128)(2,1)}), bf16[128,8,128]{2,1,0:T(8,128)(2,1)S(1)}, u32[]{:S(2)}, u32[]{:S(2)}) async-start(bf16[128,8,128]{2,1,0:T(8,128)(2,1)} %pack.1), calls=%async_computation | async-start | bytes 524288 | tf_op jit(solution)/shard_map/all_to_all | solution.py:217
  19.4 0.0 copy-start.3
  19.4 0.7 %copy-done.3 = s32[2,64]{1,0:T(2,128)S(1)} copy-done((s32[2,64]{1,0:T(2,128)S(1)}, s32[2,64]{1,0:T(2,128)}, u32[]{:S(2)}) %copy-start.3) | copy-done | bytes 536
  20.1 0.0 copy-start.4
  20.1 0.7 %copy-done.4 = s32[2,64]{1,0:T(2,128)S(1)} copy-done((s32[2,64]{1,0:T(2,128)S(1)}, s32[2,64]{1,0:T(2,128)}, u32[]{:S(2)}) %copy-start.4) | copy-done | bytes 536
  20.8 0.0 copy-start.5
  20.8 4.5 %tiles.1 = (s8[80,128,256]{2,1,0:T(32,128)(4,1)S(1)}, s32[2,64]{1,0:T(2,128)S(1)}, s32[2,64]{1,0:T(2,128)S(1)}) custom-call(s32[2,64,128,128]{3,2,1,0:T(8,128)} %tiles_ref.1, s32[2,64]{1,0:T(2,128)S(1)} %copy-done.3, s32[2,64]{1,0:T(2,128)S(1)} %copy-done.4), custom_call_target="tpu_custom_call" | custom-call | bytes 13631488 | tf_op jit(solution)/shard_map/tiles/pallas_call | solution.py:221
  25.3 0.0 copy-start.1
  25.3 0.5 all-to-all-done.panels_ref
  25.8 0.0 copy-done.5
  25.8 2.4 %slots.1 = (bf16[128,4,384]{2,1,0:T(4,128)(2,1)}, f32[8,128]{1,0:T(8,128)S(1)}) custom-call(s32[2,64]{1,0:T(2,128)S(1)} %get-tuple-element.12.rows_hbm, s32[2,64]{1,0:T(2,128)S(1)} %get-tuple-element.13.cols_hbm, s32[2]{0:T(128)S(1)} %copy-done.5, bf16[128,8,128]{2,1,0:T(8,128)(2,1)S(1)} %all-to-all-done.panels_ref, ...), custom_call_target="tpu_custom_call" | custom-call | tf_op jit(solution)/shard_map/slots/pallas_call | solution.py:238
  28.2 13.2 %all-to-all-start.1 = ((bf16[128,4,384]{2,1,0:T(4,128)(2,1)}), bf16[128,4,384]{2,1,0:T(4,128)(2,1)S(1)}, u32[]{:S(2)}, u32[]{:S(2)}) async-start(bf16[128,4,384]{2,1,0:T(4,128)(2,1)} %get-tuple-element.17), calls=%async_computation.1 | async-start | bytes 786432 | tf_op jit(solution)/shard_map/all_to_all | solution.py:256
  41.4 0.0 copy-done.1
  41.4 0.0 copy-start
  41.4 1.7 %copy-done = bf16[2,768,768]{2,1,0:T(8,128)(2,1)S(1)} copy-done((bf16[2,768,768]{2,1,0:T(8,128)(2,1)S(1)}, bf16[2,768,768]{2,1,0:T(8,128)(2,1)}, u32[]{:S(2)}) %copy-start) | copy-done | bytes 2359320
  43.1 0.0 copy-start.2
  43.1 1.1 %copy-done.2 = bf16[384,768]{1,0:T(8,128)(2,1)S(1)} copy-done((bf16[384,768]{1,0:T(8,128)(2,1)S(1)}, bf16[384,768]{1,0:T(8,128)(2,1)}, u32[]{:S(2)}) %copy-start.2) | copy-done | bytes 589848
  44.1 2.3 %weights.1 = (bf16[768,1536]{1,0:T(8,128)(2,1)S(1)}, f32[768,128]{1,0:T(8,128)S(1)}) custom-call(bf16[2,768,768]{2,1,0:T(8,128)(2,1)S(1)} %copy-done, bf16[384,768]{1,0:T(8,128)(2,1)S(1)} %copy-done.2, bf16[768,128]{1,0:T(8,128)(2,1)S(1)} %copy-done.1, f32[8,128]{1,0:T(8,128)S(1)} %get-tuple-element.15.token_ref), custom_call_target="tpu_custom_call" | custom-call | flops 100000000 | bytes 7340032 | tf_op jit(solution)/shard_map/weights/pallas_call | solution.py:259
  46.5 3.7 %all-to-all-done.1.hidden_ref = bf16[128,4,384]{2,1,0:T(4,128)(2,1)S(1)} async-done(((bf16[128,4,384]{2,1,0:T(4,128)(2,1)}), bf16[128,4,384]{2,1,0:T(4,128)(2,1)S(1)}, u32[]{:S(2)}, u32[]{:S(2)}) %all-to-all-start.1) | async-done | bytes 393248 | tf_op jit(solution)/shard_map/all_to_all | solution.py:256
  50.1 0.8 %transform.1 = f32[768,128]{1,0:T(8,128)S(1)} custom-call(bf16[768,1536]{1,0:T(8,128)(2,1)S(1)} %get-tuple-element.16.turned_ref, bf16[128,4,384]{2,1,0:T(4,128)(2,1)S(1)} %all-to-all-done.1.hidden_ref, f32[768,128]{1,0:T(8,128)S(1)} %get-tuple-element.18.own_ref), custom_call_target="tpu_custom_call" | custom-call | tf_op jit(solution)/shard_map/transform/pallas_call | solution.py:271
  51.0 1.6 %collective-permute-start = (f32[768,128]{1,0:T(8,128)S(1)}, f32[768,128]{1,0:T(8,128)S(1)}, u32[]{:S(2)}, u32[]{:S(2)}) collective-permute-start(f32[768,128]{1,0:T(8,128)S(1)} %transform.1), channel_id=1, source_target_pairs={{0,1},{1,0},{2,3},{3,2},{4,5},{5,4},{6,7},{7,6},{8,9},{9,8},{10,11... | collective-permute-start | bytes 1179656 | tf_op jit(solution)/shard_map/ppermute | solution.py:279
  52.6 1.3 %collective-permute-done = f32[768,128]{1,0:T(8,128)S(1)} collective-permute-done((f32[768,128]{1,0:T(8,128)S(1)}, f32[768,128]{1,0:T(8,128)S(1)}, u32[]{:S(2)}, u32[]{:S(2)}) %collective-permute-start) | collective-permute-done | bytes 393248 | tf_op jit(solution)/shard_map/ppermute | solution.py:279
  53.9 0.7 %maximum_convert_fusion = bf16[768,128]{1,0:T(8,128)(2,1)} fusion(f32[768,128]{1,0:T(8,128)S(1)} %transform.1, f32[768,128]{1,0:T(8,128)S(1)} %collective-permute-done), kind=kLoop, calls=%fused_computation | loop fusion | flops 294912 | bytes 983040 | tf_op jit(solution)/shard_map/convert_element_type | solution.py:280
Async XLA Ops:
  1.8 24.0 %all-to-all-start = ((bf16[128,8,128]{2,1,0:T(8,128)(2,1)}), bf16[128,8,128]{2,1,0:T(8,128)(2,1)S(1)}, u32[]{:S(2)}, u32[]{:S(2)}) async-start(bf16[128,8,128]{2,1,0:T(8,128)(2,1)} %pack.1), calls=%async_computation | async-start | bytes 524288 | tf_op jit(solution)/shard_map/all_to_all | solution.py:217
  19.4 0.7 %copy-start.3 = (s32[2,64]{1,0:T(2,128)S(1)}, s32[2,64]{1,0:T(2,128)}, u32[]{:S(2)}) copy-start(s32[2,64]{1,0:T(2,128)} %rows_ref.1) | copy-start | bytes 1540
  20.1 0.7 %copy-start.4 = (s32[2,64]{1,0:T(2,128)S(1)}, s32[2,64]{1,0:T(2,128)}, u32[]{:S(2)}) copy-start(s32[2,64]{1,0:T(2,128)} %cols_ref.1) | copy-start | bytes 1540
  20.8 5.0 %copy-start.5 = (s32[2]{0:T(128)S(1)}, s32[2]{0:T(128)}, u32[]{:S(2)}) copy-start(s32[2]{0:T(128)} %live_hbm.1) | copy-start | bytes 28
  25.3 16.1 %copy-start.1 = (bf16[768,128]{1,0:T(8,128)(2,1)S(1)}, bf16[768,128]{1,0:T(8,128)(2,1)}, u32[]{:S(2)}) copy-start(bf16[768,128]{1,0:T(8,128)(2,1)} %features_ref.3) | copy-start | bytes 589828
  28.2 21.9 %all-to-all-start.1 = ((bf16[128,4,384]{2,1,0:T(4,128)(2,1)}), bf16[128,4,384]{2,1,0:T(4,128)(2,1)S(1)}, u32[]{:S(2)}, u32[]{:S(2)}) async-start(bf16[128,4,384]{2,1,0:T(4,128)(2,1)} %get-tuple-element.17), calls=%async_computation.1 | async-start | bytes 786432 | tf_op jit(solution)/shard_map/all_to_all | solution.py:256
  41.4 1.7 %copy-start = (bf16[2,768,768]{2,1,0:T(8,128)(2,1)S(1)}, bf16[2,768,768]{2,1,0:T(8,128)(2,1)}, u32[]{:S(2)}) copy-start(bf16[2,768,768]{2,1,0:T(8,128)(2,1)} %rel_ref.1) | copy-start | bytes 7077892
  43.1 1.1 %copy-start.2 = (bf16[384,768]{1,0:T(8,128)(2,1)S(1)}, bf16[384,768]{1,0:T(8,128)(2,1)}, u32[]{:S(2)}) copy-start(bf16[384,768]{1,0:T(8,128)(2,1)} %self_ref.1) | copy-start | bytes 1769476
  51.0 2.9 %collective-permute-start = (f32[768,128]{1,0:T(8,128)S(1)}, f32[768,128]{1,0:T(8,128)S(1)}, u32[]{:S(2)}, u32[]{:S(2)}) collective-permute-start(f32[768,128]{1,0:T(8,128)S(1)} %transform.1), channel_id=1, source_target_pairs={{0,1},{1,0},{2,3},{3,2},{4,5},{5,4},{6,7},{7,6},{8,9},{9,8},{10,11... | collective-permute-start | bytes 1179656 | tf_op jit(solution)/shard_map/ppermute | solution.py:279
